TPU v7x, 32 devices: a whole 2x2x4 slice. The times are simulated.
32 devices in a mesh: dp: 8 (over z, y), expert: 4 (over x, core).
Axes of the slice: x: 2, y: 2, z: 4, core: 2. Of those that a mesh axis runs over, the one named last changes fastest.
Arguments:
- tokens: bfloat16 [4096, 1536], P(('dp', 'expert')), may hold values from -6 to 6
- segments: int32 [32, 128], P(('dp', 'expert')), may hold values from 0 to 3, never falling along the last dimension, each value on 1 to 64 neighbouring positions
- routes: int32 [4096, 8], P(('dp', 'expert')), may hold values from 0 to 39, all different within a row; in each aligned block of 128 rows (0 to 127, 128 to 255, ...) at most 40 rows name the same one
- w_query: bfloat16 [1536, 1536], P('dp'), may hold values from -0.15625 to 0.15625
- w_key: bfloat16 [1536, 512], P('dp'), may hold values from -0.15625 to 0.15625
- w_value: bfloat16 [1536, 512], P('dp'), may hold values from -0.15625 to 0.15625
- w_output: bfloat16 [1536, 1536], P('dp'), may hold values from -0.625 to 0.625
- w_router: bfloat16 [1536, 40], P('dp'), may hold values from -0.078125 to 0.078125
- gain_attn: bfloat16 [1536], P('dp'), may hold values from 0.099609375 to 1.8984375
- gain_moe: bfloat16 [1536], P('dp'), may hold values from 0.099609375 to 1.8984375
- w_gate_up: bfloat16 [40, 1536, 1024], P('expert'), may hold values from -0.15625 to 0.15625
- w_down: bfloat16 [40, 512, 1536], P('expert'), may hold values from -1 to 1
- cotangent: bfloat16 [4096, 1536], P(('dp', 'expert')), may hold values from -6 to 6
Outputs:
- output: bfloat16 [4096, 1536], P(('dp', 'expert'))
- grad_tokens: bfloat16 [4096, 1536], P(('dp', 'expert'))
- grad_query: float32 [1536, 1536], P('dp')
- grad_key: float32 [1536, 512], P('dp')
- grad_value: float32 [1536, 512], P('dp')
- grad_output: float32 [1536, 1536], P('dp')
- grad_router: float32 [1536, 40], P('dp')
- grad_gain_attn: float32 [1536], P('dp')
- grad_gain_moe: float32 [1536], P('dp')
- grad_gate_up: float32 [40, 1536, 1024], P('expert', 'dp')
- grad_down: float32 [40, 512, 1536], P('expert', 'dp')
Inputs may be any that keep to these rules, and one draw needn't show every extreme that they name: `routes`: in each aligned block of 128 rows (the rows of one device) no expert is named by more than 40 rows, a bound that some block reaches; the 8 experts of a row differ. `segments`: along each row the numbers never fall; a segment spans at most half of 128 positions, some segment exactly that.
All inputs are finite; a program needn't handle non-finite values.
Results may differ from a plain program's by a relative error of at most 0.023.
Values may be sent and summed in bfloat16 or wider, within the bound.
A program may use at most 256 MiB of HBM per device.

v0:
```python
import functools

import jax
import jax.numpy as jnp
import numpy as np
from jax import lax
from jax.experimental import pallas as pl
from jax.experimental.pallas import tpu as pltpu
from jax.sharding import PartitionSpec as P

H = 24
KV = 8
HD = 64
F = 512
EXPERTS = 40
ZLINE = 4
GROUP = 2


epsilon = 1e-05
f32 = jnp.float32
bf16 = jnp.bfloat16


def tables(length, size):
    half_size = size // 2
    frequency = jnp.power(10000.0, -2.0 * jnp.arange(half_size, dtype=f32) / size)
    angles = jnp.arange(length, dtype=f32)[:, None] * frequency[None, :]
    return (jnp.cos(angles)[:, None, :], jnp.sin(angles)[:, None, :])


def rotate(source, cosine_table, sine_table):
    half_size = source.shape[-1] // 2
    first_half = source[..., :half_size]
    second_half = source[..., half_size:]
    return jnp.concatenate(
        [
            first_half * cosine_table - second_half * sine_table,
            second_half * cosine_table + first_half * sine_table,
        ],
        axis=-1,
    )


def dot(left_side, right_side):
    return jnp.dot(left_side, right_side, preferred_element_type=f32)


def transposed(left_side, right_side):
    return lax.dot_general(
        left_side, right_side, (((0,), (0,)), ((), ())), preferred_element_type=f32
    )


def against(left_side, right_side):
    return lax.dot_general(
        left_side, right_side, (((1,), (1,)), ((), ())), preferred_element_type=f32
    )


def swap(value, axis, mask):
    size = lax.axis_size(axis)
    return lax.ppermute(value, axis, [(i, i ^ mask) for i in range(size)])


def pick(value, at):
    return lax.dynamic_index_in_dim(value, at, 0, keepdims=False)


def bits(first, size):
    masks, step = [], 1
    while step < size:
        masks.append(first * step)
        step *= 2
    return masks


class Place:
    def __init__(self):
        self.dp_size = lax.axis_size("dp")
        self.ex_size = lax.axis_size("expert")
        self.dp = lax.axis_index("dp")
        self.ex = lax.axis_index("expert")
        self.rows_y = self.dp_size // ZLINE
        self.z = self.dp // self.rows_y
        self.y = self.dp % self.rows_y
        self.z_bits = bits(self.rows_y, ZLINE)
        self.y_bits = bits(1, self.rows_y)
        self.x_bits = bits(2, self.ex_size // 2)


def gather_weights(place, shard):
    n, columns = shard.shape
    piece = n // 6
    cut = shard.reshape(3, 2, piece, columns)
    core = place.ex % 2
    side = (place.ex // 2) % 2
    own = pick(cut.swapaxes(0, 1), core)
    sibling = pick(cut.swapaxes(0, 1), 1 - core)

    def ordered(parts):
        return jnp.stack([pick(parts, 2 * side), parts[1], pick(parts, 2 - 2 * side)])

    own, sibling = ordered(own), ordered(sibling)
    blocks = {0: own[:2]}
    for mask in place.z_bits + place.y_bits:
        blocks.update({m ^ mask: swap(v, "dp", mask) for m, v in list(blocks.items())})
    rows = []
    for m in range(place.dp_size):
        if m == 0:
            rows.append(jnp.stack([own, sibling], axis=1))
            continue
        other = swap(blocks[m][0], "expert", 2)
        trio = jnp.concatenate([blocks[m], other[None]], axis=0)
        rows.append(jnp.stack([trio, swap(trio, "expert", 1)], axis=1))
    full = jnp.stack(rows)
    total = place.dp_size * n
    k = jnp.arange(total, dtype=jnp.int32)
    block, part = k // n, (k % n) // (2 * piece)
    half, line = (k % (2 * piece)) // piece, k % piece
    part = jnp.where(part == 1, 1, jnp.where(part == 0, 2 * side, 2 - 2 * side))
    at = (block ^ place.dp) * n + part * 2 * piece + (half ^ core) * piece + line
    order = (at[:, None] == jnp.arange(total, dtype=jnp.int32)[None, :]).astype(bf16)
    return full.reshape(total, columns), order


def scatter_weights(place, part):
    total, columns = part.shape
    n = total // place.dp_size
    piece = n // 6
    core = place.ex % 2
    side = (place.ex // 2) % 2

    def add(left, right):
        return (left.astype(f32) + right.astype(f32)).astype(bf16)

    part = part.reshape(place.dp_size, 3, 2, piece, columns)
    kept = add(part[:, :, 0], swap(part[:, :, 1], "expert", 1))
    first = add(kept[:, 0], swap(kept[:, 2], "expert", 2))
    blocks = {m: jnp.stack([first[m], kept[m, 1]]) for m in range(place.dp_size)}
    for mask in (place.z_bits + place.y_bits)[::-1]:
        blocks = {
            m: add(v, swap(blocks[m ^ mask], "dp", mask))
            for m, v in blocks.items()
            if m & mask == 0
        }
    mine = blocks[0]
    middle = add(mine[1], swap(mine[1], "expert", 2))
    trio = jnp.stack([mine[0], middle, swap(mine[0], "expert", 2)])
    for mask in place.x_bits[1:]:
        trio = add(trio, swap(trio, "expert", mask))
    both = jnp.stack([trio, swap(trio, "expert", 1)], axis=1)
    both = jnp.where(side == 0, both, both[::-1])
    both = jnp.where(core == 0, both, both[:, ::-1])
    return both.reshape(n, columns).astype(f32)


def gather_tokens(place, block):
    blocks = {0: block}
    for mask in place.z_bits:
        blocks.update({m ^ mask: swap(v, "dp", mask) for m, v in list(blocks.items())})
    groups = []
    for r in range(ZLINE):
        row = [blocks[r * place.rows_y]]
        for mask in place.x_bits:
            row = row + [swap(v, "expert", mask) for v in row]
        row = jnp.concatenate(row, axis=0)
        groups.append(jnp.concatenate([row, swap(row, "expert", 1)], axis=0))
    return groups


def scatter_tokens(place, groups, length):
    def add(left, right):
        return left.astype(f32) + right.astype(f32)

    reduced = []
    for part in groups:
        half = part.shape[0] // 2
        kept = add(part[:half], swap(part[half:], "expert", 1)).astype(bf16)
        for mask in place.x_bits[::-1]:
            half = kept.shape[0] // 2
            kept = add(kept[:half], swap(kept[half:], "expert", mask)).astype(bf16)
        reduced.append(kept)
    two = [add(reduced[i], swap(reduced[i + 2], "dp", place.z_bits[1])) for i in range(2)]
    return add(two[0], swap(two[1].astype(bf16), "dp", place.z_bits[0]))


def other(index, mask):
    return index + mask - 2 * mask * ((index // mask) % 2)


class Links:
    def __init__(self, sends, recvs):
        self.sends, self.recvs, self.used, self.open = sends, recvs, 0, []

    def copy(self, source, target, partner):
        at = self.used
        self.used += 1
        made = pltpu.make_async_remote_copy(
            src_ref=source,
            dst_ref=target,
            send_sem=self.sends.at[at],
            recv_sem=self.recvs.at[at],
            device_id=partner,
            device_id_type=pl.DeviceIdType.MESH,
        )
        made.start()
        self.open.append(made)
        return made

    def close(self):
        for made in self.open:
            made.wait_send()


def partners(rows_y):
    dp, ex = lax.axis_index("dp"), lax.axis_index("expert")
    return {
        "z1": (other(dp, rows_y), ex),
        "z2": (other(dp, 2 * rows_y), ex),
        "y": (other(dp, 1), ex),
        "x": (dp, other(ex, 2)),
        "c": (dp, other(ex, 1)),
    }


def greet(devices):
    barrier = pltpu.get_barrier_semaphore()
    for device in devices:
        pl.semaphore_signal(
            barrier, inc=1, device_id=device, device_id_type=pl.DeviceIdType.MESH
        )
    pl.semaphore_wait(barrier, len(devices))


def gather_kernel(
    rows_y,
    exclusive,
    w_query,
    w_key,
    w_value,
    w_output,
    w_router,
    gain_attn,
    gain_moe,
    dy,
    tokens_ref,
    segments,
    routes,
    cosine,
    sine,
    down_hbm,
    qkv_out,
    output_out,
    dy_out,
    grads_out,
    small_out,
    queries_out,
    keys_out,
    values_out,
    residual_out,
    normed_moe_out,
    normed_turned,
    mixed_turned,
    gains_out,
    gates_out,
    allowed,
    full_qkv,
    full_output,
    dy_all,
    w_down,
    grads,
    projected,
    normed_out,
    mixed_out,
    *refs,
):
    z_send, z_recv, y_send, y_recv, x_send, x_recv, c_send, c_recv = refs[:8]
    dz_send, dz_recv, dx_send, dx_recv, dc_send, dc_recv, down_sem, dy_sems, grads_sems, keep_sems = refs[8:]
    fulls = (full_qkv, small_out, full_output)
    n = w_query.shape[0]
    half = n // 2
    piece = half - exclusive
    length = dy.shape[0]
    owned, hidden, width = w_down.shape
    dp, ex = lax.axis_index("dp"), lax.axis_index("expert")
    z, y = dp // rows_y, dp % rows_y
    core, side = ex % 2, (ex // 2) % 2
    to = partners(rows_y)
    z_of = [z, other(z, 1), other(z, 2), other(other(z, 1), 2)]

    in_plane = pl.ds(pl.multiple_of(core * half + side * exclusive, 16), piece)
    alone = pl.ds(pl.multiple_of(core * half + side * piece, 16), exclusive)
    of_core = pl.ds(pl.multiple_of(core * half, 16), half)

    def remote(source, target, send_sem, recv_sem, device):
        return pltpu.make_async_remote_copy(
            src_ref=source,
            dst_ref=target,
            send_sem=send_sem,
            recv_sem=recv_sem,
            device_id=device,
            device_id_type=pl.DeviceIdType.MESH,
        )

    first, second = (0, 1), (2,)

    def copies(arrays, rows, m, ys, send, recv, at, device):
        made = []
        for k in arrays:
            block = fulls[k].at[z_of[m] * rows_y + ys, rows]
            made.append(remote(block, block, send.at[k, at], recv.at[k, at], device))
        return made

    def to_z(arrays, step):
        m, device = ((0, "z1"), (0, "z2"), (2, "z1"))[step]
        return copies(arrays, in_plane, m, y, z_send, z_recv, step, to[device])

    def to_y(arrays, m):
        return copies(arrays, in_plane, m, y, y_send, y_recv, m, to["y"])

    def to_x(arrays, m, k):
        ys = 1 - y if k else y
        return copies(arrays, alone, m, ys, x_send, x_recv, 2 * m + k, to["x"])

    def to_c(arrays, m, k):
        ys = 1 - y if k else y
        return copies(arrays, of_core, m, ys, c_send, c_recv, 2 * m + k, to["c"])

    near, pair = pl.ds(0, length), pl.ds(length, length)
    front, back = pl.ds(0, 2 * length), pl.ds(2 * length, 2 * length)

    def dy_z(step):
        m, target, device = ((0, 1, "z1"), (0, 2, "z2"), (2, 3, "z1"))[step]
        return remote(
            dy_all.at[m, near], dy_all.at[target, near], dz_send.at[step], dz_recv.at[step], to[device]
        )

    def dy_x(m):
        return remote(
            dy_all.at[m, near], dy_all.at[m, pair], dx_send.at[m], dx_recv.at[m], to["x"]
        )

    def dy_c(m):
        return remote(
            dy_all.at[m, front], dy_all.at[m, back], dc_send.at[m], dc_recv.at[m], to["c"]
        )

    at = pl.ds(pl.multiple_of(z * hidden, hidden), hidden)
    load_down = pltpu.make_async_copy(down_hbm.at[:, at, :], w_down, down_sem)
    load_down.start()

    def iota(shape, axis):
        return lax.broadcasted_iota(jnp.int32, shape, axis)

    full_qkv[dp, :, : H * HD] = w_query[...]
    full_qkv[dp, :, H * HD : (H + KV) * HD] = w_key[...]
    full_qkv[dp, :, (H + KV) * HD :] = w_value[...]
    full_output[dp] = w_output[...]
    line = iota((8, n), 0)
    gain_rows = jnp.where(
        line == 0,
        gain_attn[...].astype(f32),
        jnp.where(line == 1, gain_moe[...].astype(f32), 0.0),
    ).astype(bf16)
    places = (iota((8, 128), 1) == iota((8, 128), 0) + EXPERTS) & (iota((8, 128), 0) < 2)
    columns = transposed(gain_rows, places.astype(f32).astype(bf16))
    router = jnp.concatenate(
        [w_router[...].astype(f32), jnp.zeros((n, 128 - EXPERTS), f32)], axis=1
    )
    small_out[dp] = (router + columns).astype(bf16)
    lane, row = iota((length, 128), 1), iota((length, 128), 0)
    chosen = routes[:, :1] == lane
    for k in range(1, routes.shape[1]):
        chosen = chosen | (routes[:, k : k + 1] == lane)
    chosen = chosen.astype(f32)
    dy_all[0, near, :width] = dy[...]
    dy_all[0, near, width:] = chosen.astype(bf16)
    greet([to[name] for name in ("z1", "z2", "y", "x", "c")])

    def start(made):
        for copy in made:
            copy.start()

    def arrived(made):
        for copy in made:
            copy.wait_recv()

    def keep_dy(m):
        return pltpu.make_async_copy(dy_all.at[m], dy_out.at[m], dy_sems.at[m])

    def keep_grads(m):
        return pltpu.make_async_copy(grads.at[m % 2], grads_out.at[m], grads_sems.at[m % 2])

    keep_qkv = pltpu.make_async_copy(full_qkv, qkv_out, keep_sems.at[0])
    keep_output = pltpu.make_async_copy(full_output, output_out, keep_sems.at[1])

    def group(m):
        dy_c(m).wait_recv()
        keep_dy(m).start()
        if m >= 2:
            keep_grads(m - 2).wait()

        def step(p, _):
            at = pl.ds(pl.multiple_of(p * 2 * hidden, 2 * hidden), 2 * hidden)
            down = w_down[pl.ds(2 * p, 2)].reshape(2 * hidden, width)
            grads[m % 2, :, at] = against(dy_all[m, :, :width], down).astype(bf16)
            return 0

        lax.fori_loop(0, owned // 2, step, 0)
        keep_grads(m).start()

    def turned(value, target):
        target[...] = value.T.reshape(target.shape)

    def rotated(value):
        lanes = value.shape[1]
        lane = lax.broadcasted_iota(jnp.int32, value.shape, 1)
        swapped = jnp.where(
            lane % HD < HD // 2,
            pltpu.roll(value, lanes - HD // 2, 1),
            pltpu.roll(value, HD // 2, 1),
        )
        return (value * cosine[:, :lanes] - swapped * sine[:, :lanes]).astype(bf16)

    per_group = H // KV
    wide = GROUP * per_group * HD
    narrow = GROUP * HD

    def project():
        inputs = tokens_ref[...].astype(f32)
        inv = lax.rsqrt(jnp.mean(inputs * inputs, axis=-1, keepdims=True) + epsilon)
        gains_out[...] = against(
            places.astype(f32).astype(bf16), small_out[...].reshape(width, 128)
        )
        normed_out[...] = (inputs * inv * gains_out[:1]).astype(bf16)
        segment = segments[...].astype(f32)
        same = against(
            (row == lane).astype(f32).astype(bf16), jnp.broadcast_to(segment, (8, length)).astype(bf16)
        )[:, :1]
        allowed[...] = ((same == segment) & (row >= lane)).astype(f32)

        def step(j, _):
            at = pl.ds(pl.multiple_of(j * 512, 512), 512)
            projected[:, at] = jnp.dot(
                normed_out[...], full_qkv[:, :, at].reshape(width, 512), preferred_element_type=f32
            )
            return 0

        lax.fori_loop(0, projected.shape[1] // 512, step, 0)

    def attend(i):
        at = pl.ds(i * wide, wide)
        kv_at = pl.ds(i * narrow, narrow)
        k_at = pl.ds(H * HD + i * narrow, narrow)
        v_at = pl.ds((H + KV) * HD + i * narrow, narrow)
        query = rotated(projected[:, at])
        key = rotated(projected[:, k_at])
        value = projected[:, v_at].astype(bf16)
        queries_out[:, at] = query
        keys_out[:, kv_at] = key
        values_out[:, kv_at] = value
        is_allowed = allowed[...] > 0.5
        heads = []
        for k in range(GROUP):
            k_head, v_head = key[:, k * HD : (k + 1) * HD], value[:, k * HD : (k + 1) * HD]
            for j in range(k * per_group, (k + 1) * per_group):
                q_head = query[:, j * HD : (j + 1) * HD]
                scores = jnp.where(is_allowed, against(q_head, k_head) * 0.125, -1e30)
                lifted = jnp.exp(scores - jnp.max(scores, axis=-1, keepdims=True))
                weights = (lifted / jnp.sum(lifted, axis=-1, keepdims=True)).astype(bf16)
                heads.append(jnp.dot(weights, v_head, preferred_element_type=f32))
        mixed_out[:, at] = jnp.concatenate(heads, axis=1).astype(bf16)

    def close_block():
        def step(j, _):
            at = pl.ds(pl.multiple_of(j * 512, 512), 512)
            residual_out[:, at] = tokens_ref[:, at].astype(f32) + jnp.dot(
                mixed_out[...], full_output[:, :, at].reshape(width, 512), preferred_element_type=f32
            )
            return 0

        lax.fori_loop(0, width // 512, step, 0)
        residual = residual_out[...]
        inv = lax.rsqrt(jnp.mean(residual * residual, axis=-1, keepdims=True) + epsilon)
        normed_moe_out[...] = (residual * inv * gains_out[1:2]).astype(bf16)
        logits = jnp.dot(
            normed_moe_out[...], small_out[...].reshape(width, 128), preferred_element_type=f32
        )
        logits = jnp.where(chosen > 0.5, logits, -1e30)
        lifted = jnp.exp(logits - jnp.max(logits, axis=-1, keepdims=True)) * chosen
        gates_out[...] = lifted / jnp.sum(lifted, axis=-1, keepdims=True)
        turned(mixed_out[...], mixed_turned)

    start(to_z(first, 1))
    start(to_z(first, 0))
    start(to_y(first, 0))
    dy_x(0).start()

    arrived(to_z(first, 0))
    start(to_y(first, 1))
    start(to_x(first, 1, 0))
    arrived(to_z(first, 1))
    start(to_z(first, 2))
    start(to_y(first, 2))
    start(to_x(first, 2, 0))
    start(to_z(second, 1))
    start(to_z(second, 0))
    start(to_y(second, 0))
    dy_x(0).wait_recv()
    dy_c(0).start()
    arrived(to_y(first, 0))
    start(to_x(first, 0, 1))
    load_down.wait()
    group(0)
    arrived(to_z(first, 2))
    start(to_y(first, 3))
    start(to_x(first, 3, 0))
    arrived(to_z(second, 0))
    start(to_y(second, 1))
    start(to_x(second, 1, 0))
    arrived(to_z(second, 1))
    start(to_z(second, 2))
    start(to_y(second, 2))
    start(to_x(second, 2, 0))
    dy_z(1).start()
    dy_z(0).start()
    arrived(to_y(first, 1))
    start(to_x(first, 1, 1))
    arrived(to_y(first, 2))
    start(to_x(first, 2, 1))
    for m, k in ((1, 0), (2, 0), (0, 1), (3, 0), (1, 1)):
        arrived(to_x(first, m, k))
        start(to_c(first, m, k))
    arrived(to_y(first, 3))
    start(to_x(first, 3, 1))
    arrived(to_x(first, 2, 1))
    start(to_c(first, 2, 1))
    arrived(to_z(second, 2))
    start(to_y(second, 3))
    start(to_x(second, 3, 0))
    arrived(to_y(second, 0))
    start(to_x(second, 0, 1))
    arrived(to_x(first, 3, 1))
    start(to_c(first, 3, 1))
    for m, k in ((1, 0), (2, 0), (0, 1), (3, 0), (1, 1), (2, 1), (3, 1)):
        arrived(to_c(first, m, k))
    keep_qkv.start()
    project()
    turned(normed_out[...], normed_turned)
    arrived(to_y(second, 1))
    start(to_x(second, 1, 1))
    arrived(to_y(second, 2))
    start(to_x(second, 2, 1))
    dy_z(0).wait_recv()
    dy_x(1).start()
    attend(0)
    dy_z(1).wait_recv()
    dy_z(2).start()
    dy_x(2).start()
    attend(1)
    for m, k in ((1, 0), (2, 0), (0, 1), (3, 0), (1, 1), (2, 1)):
        arrived(to_x(second, m, k))
        start(to_c(second, m, k))
    arrived(to_y(second, 3))
    start(to_x(second, 3, 1))
    attend(2)
    dy_x(1).wait_recv()
    dy_c(1).start()
    attend(3)
    arrived(to_x(second, 3, 1))
    start(to_c(second, 3, 1))
    group(1)
    dy_z(2).wait_recv()
    dy_x(3).start()
    for m, k in ((1, 0), (2, 0), (0, 1), (3, 0), (1, 1), (2, 1), (3, 1)):
        arrived(to_c(second, m, k))
    keep_output.start()
    close_block()
    dy_x(2).wait_recv()
    dy_c(2).start()
    group(2)
    dy_x(3).wait_recv()
    dy_c(3).start()
    group(3)

    keep_qkv.wait()
    keep_output.wait()
    for m in range(ZLINE):
        keep_dy(m).wait()
        if m >= 2:
            keep_grads(m).wait()
    every = first + second
    for step in range(3):
        for made in to_z(every, step):
            made.wait_send()
        dy_z(step).wait_send()
    for m in range(ZLINE):
        for made in to_y(every, m):
            made.wait_send()
        dy_x(m).wait_send()
        dy_c(m).wait_send()
        for k in range(2):
            if m or k:
                for made in to_x(every, m, k) + to_c(every, m, k):
                    made.wait_send()


def gather(rows_y, weights, dy, *rest):
    w_down = rest[-1]
    n, router_wide = weights[4].shape
    dp_size = ZLINE * rows_y
    owned, _, width = w_down.shape
    hidden = F // ZLINE
    length = dy.shape[0]
    count = 4 * length
    qkv_wide = weights[0].shape[1] + weights[1].shape[1] + weights[2].shape[1]
    any_space = pl.BlockSpec(memory_space=pl.ANY)
    vmem = pl.BlockSpec(memory_space=pltpu.VMEM)
    sems = pltpu.SemaphoreType.DMA

    def rows(wide, dtype=bf16):
        return jax.ShapeDtypeStruct((length, wide), dtype)

    turned = jax.ShapeDtypeStruct((dp_size, 2, 2, n // 4, length), bf16)
    return pl.pallas_call(
        functools.partial(gather_kernel, rows_y, n // 12),
        name="gather",
        out_shape=(
            jax.ShapeDtypeStruct((dp_size, n, qkv_wide), bf16),
            jax.ShapeDtypeStruct((dp_size, n, width), bf16),
            jax.ShapeDtypeStruct((ZLINE, count, width + 128), bf16),
            jax.ShapeDtypeStruct((ZLINE, count, owned * hidden), bf16),
            jax.ShapeDtypeStruct((dp_size, n, 128), bf16),
            rows(H * HD),
            rows(KV * HD),
            rows(KV * HD),
            rows(width, f32),
            rows(width),
            turned,
            turned,
            jax.ShapeDtypeStruct((8, width), f32),
            rows(128, f32),
            rows(length, f32),
        ),
        in_specs=[vmem] * (len(weights) + len(rest)) + [any_space],
        out_specs=(any_space,) * 4 + (vmem,) * 11,
        scratch_shapes=[
            pltpu.VMEM((dp_size, n, qkv_wide), bf16),
            pltpu.VMEM((dp_size, n, width), bf16),
            pltpu.VMEM((ZLINE, count, width + 128), bf16),
            pltpu.VMEM((owned, hidden, width), bf16),
            pltpu.VMEM((2, count, owned * hidden), bf16),
            pltpu.VMEM((length, qkv_wide), f32),
            pltpu.VMEM((length, width), bf16),
            pltpu.VMEM((length, H * HD), bf16),
            sems((3, 3)),
            sems((3, 3)),
            sems((3, ZLINE)),
            sems((3, ZLINE)),
            sems((3, dp_size)),
            sems((3, dp_size)),
            sems((3, dp_size)),
            sems((3, dp_size)),
            sems((3,)),
            sems((3,)),
            sems((ZLINE,)),
            sems((ZLINE,)),
            sems((ZLINE,)),
            sems((ZLINE,)),
            sems,
            sems((ZLINE,)),
            sems((2,)),
            sems((2,)),
        ],
        compiler_params=pltpu.CompilerParams(
            collective_id=2, has_side_effects=True, vmem_limit_bytes=60 * 2**20
        ),
    )(*weights, dy, *rest)


MOE_COPIES = 30


def moe_kernel(
    rows_y,
    normed_ref,
    dy_hbm,
    plain_hbm,
    gate_up_hbm,
    down_hbm,
    router_ref,
    rows_out,
    grads_out,
    down_out,
    combined_out,
    heard_out,
    total_ref,
    w_gate,
    w_up,
    w_down,
    rows,
    masks,
    plain,
    grads,
    acts,
    gate_grads,
    part_down,
    heard_down,
    stage_down,
    parts,
    heard_c,
    heard_x,
    heard_z,
    combined,
    heard_combined,
    spread_ref,
    sends,
    recvs,
    d_send,
    d_recv,
    load_sems,
    plain_sems,
    dy_sems,
    rows_sems,
    grads_sems,
    down_sems,
    combined_sems,
):
    owned, hidden = w_down.shape[:2]
    length, width = normed_ref.shape
    count = rows.shape[1]
    tokens = ZLINE * count
    half = count // 2
    span = owned * hidden
    dp = lax.axis_index("dp")
    z, y = dp // rows_y, dp % rows_y
    to = partners(rows_y)
    to["z3"] = (other(to["z1"][0], 2 * rows_y), lax.axis_index("expert"))
    links = Links(sends, recvs)

    loads = []
    mine = pl.ds(pl.multiple_of(z * hidden, hidden), hidden)
    theirs = pl.ds(pl.multiple_of(F + z * hidden, hidden), hidden)
    for e in range(owned):
        at = pl.ds(e * hidden, hidden)
        for k, (cut, kept) in enumerate(((mine, w_gate), (theirs, w_up))):
            loads.append(
                pltpu.make_async_copy(
                    gate_up_hbm.at[e, :, cut], kept.at[:, at], load_sems.at[2 * e + k]
                )
            )
    loads.append(
        pltpu.make_async_copy(dy_hbm.at[:, :, pl.ds(width, 128)], masks, load_sems.at[2 * owned])
    )
    load_down = pltpu.make_async_copy(
        down_hbm.at[:, mine, :], w_down, load_sems.at[2 * owned + 1]
    )
    for load in loads:
        load.start()

    def fetch(r):
        return pltpu.make_async_copy(plain_hbm.at[r], plain.at[r % 2], plain_sems.at[r % 2])

    fetch(0).start()
    fetch(1).start()
    load_down.start()
    rows[0, :length] = normed_ref[...]
    first = lax.axis_index("expert") * owned
    expert = first + lax.broadcasted_iota(jnp.int32, (128, span), 1) // hidden
    spread_ref[...] = (
        (lax.broadcasted_iota(jnp.int32, (128, span), 0) == expert).astype(f32).astype(bf16)
    )
    greet([to[name] for name in ("z1", "z2", "z3", "y", "x", "c")])

    own = pl.ds(0, length)
    pair = pl.ds(length, length)
    near, far = pl.ds(0, half), pl.ds(half, half)

    def row_x(r):
        return links.copy(rows.at[r, own], rows.at[r, pair], to["x"])

    def row_c(r):
        return links.copy(rows.at[r, near], rows.at[r, far], to["c"])

    z1 = links.copy(rows.at[0, own], rows.at[1, own], to["z1"])
    z2 = links.copy(rows.at[0, own], rows.at[2, own], to["z2"])
    x0 = row_x(0)
    for load in loads:
        load.wait()
    x0.wait_recv()
    c0 = row_c(0)
    c0.wait_recv()

    def keep_rows(r):
        return pltpu.make_async_copy(rows.at[r], rows_out.at[r], rows_sems.at[r])

    def keep_grads(r):
        return pltpu.make_async_copy(grads.at[min(r, 1)], grads_out.at[r], grads_sems.at[r])

    def forward(r):
        slot, held = r % 2, min(r, 1)
        keep_rows(r).start()
        fetch(r).wait()
        if r >= 2:
            keep_grads(r - 1).wait()
        logits = jnp.dot(rows[r], router_ref[...], preferred_element_type=f32)
        mask = masks[r].astype(f32) > 0.5
        logits = jnp.where(mask, logits, -1e30)
        lifted = jnp.where(
            mask, jnp.exp(logits - jnp.max(logits, axis=-1, keepdims=True)), 0.0
        )
        gates = lifted / jnp.sum(lifted, axis=-1, keepdims=True)
        gates_high = gates.astype(bf16)
        gates_low = (gates - gates_high.astype(f32)).astype(bf16)
        gate_grads[...] = jnp.zeros_like(gate_grads)

        def step(p, _):
            at = pl.ds(pl.multiple_of(p * 2 * hidden, 2 * hidden), 2 * hidden)
            up_at = pl.ds(pl.multiple_of(span + p * 2 * hidden, 2 * hidden), 2 * hidden)
            spread = spread_ref[:, at]
            gate_part = jnp.dot(rows[r], w_gate[:, at], preferred_element_type=f32)
            up_part = jnp.dot(rows[r], w_up[:, at], preferred_element_type=f32)
            plain_grad = plain[slot, :, at].astype(f32)
            spread_gates = jnp.dot(gates_high, spread, preferred_element_type=f32) + jnp.dot(
                gates_low, spread, preferred_element_type=f32
            )
            sigmoid_gate = 1.0 / (1.0 + jnp.exp(-gate_part))
            swished = gate_part * sigmoid_gate
            activation = swished * up_part
            gate_grads[...] += against((plain_grad * activation).astype(bf16), spread)
            acts[r, :, at] = (spread_gates * activation).astype(bf16)
            grad_act = plain_grad * spread_gates
            grads[held, :, at] = (
                grad_act * up_part * (sigmoid_gate + swished * (1.0 - sigmoid_gate))
            ).astype(bf16)
            grads[held, :, up_at] = (grad_act * swished).astype(bf16)
            return 0

        lax.fori_loop(0, owned // 2, step, 0, unroll=True)
        parts[r, :, width:] = gate_grads[...].astype(bf16)
        if r + 2 < ZLINE:
            fetch(r + 2).start()
        keep_grads(r).start()

    def backward(r):
        held = min(r, 1)

        def step(j, _):
            at = pl.ds(pl.multiple_of(j * 768, 768), 768)
            part = against(grads[held, :, :span], w_gate[at, :]) + against(
                grads[held, :, span:], w_up[at, :]
            )
            parts[r, :, at] = part.astype(bf16)
            return 0

        lax.fori_loop(0, width // 768, step, 0)

    def add(left, right):
        return (left[...].astype(f32) + right[...].astype(f32)).astype(bf16)

    made = {}

    def sum_c(r):
        made["c", r] = links.copy(parts.at[r, far], heard_c.at[r], to["c"])

    def sum_x(r):
        made["c", r].wait_recv()
        parts[r, near] = add(parts.at[r, near], heard_c.at[r])
        made["x", r] = links.copy(parts.at[r, pair], heard_x.at[r], to["x"])

    def sum_z(r):
        made["x", r].wait_recv()
        parts[r, own] = add(parts.at[r, own], heard_x.at[r])
        if r:
            made["z", r] = links.copy(parts.at[r, own], heard_z.at[r - 1], to[f"z{r}"])

    def keep_combined(r):
        return pltpu.make_async_copy(
            combined.at[r % 2, near], combined_out.at[r], combined_sems.at[r]
        )

    def combine(r):
        slot = r % 2
        if r >= 2:
            made["oc", r - 2].wait_send()
            keep_combined(r - 2).wait()
            out_x(r - 2)

        def step(j, _):
            at = pl.ds(pl.multiple_of(j * 512, 512), 512)
            down = w_down[:, :, at].reshape(span, 512)
            combined[slot, :, at] = jnp.dot(
                acts[r], down, preferred_element_type=f32
            ).astype(bf16)
            return 0

        lax.fori_loop(0, width // 512, step, 0)
        made["oc", r] = links.copy(combined.at[slot, far], heard_combined.at[r], to["c"])

    def out_c(r):
        made["oc", r].wait_recv()
        combined[r % 2, near] = add(combined.at[r % 2, near], heard_combined.at[r])
        keep_combined(r).start()

    def out_x(r):
        made["ox", r] = links.copy(combined_out.at[r, pair], heard_out.at[r], to["x"])

    def fetch_dy(r):
        return pltpu.make_async_copy(
            dy_hbm.at[r, :, pl.ds(0, width)], rows.at[r], dy_sems.at[r]
        )

    def send_down(e):
        return pltpu.make_async_remote_copy(
            src_ref=part_down.at[e, 1 - y],
            dst_ref=heard_down.at[e],
            send_sem=d_send.at[e],
            recv_sem=d_recv.at[e],
            device_id=to["y"],
            device_id_type=pl.DeviceIdType.MESH,
        )

    def down(p, _):
        at = pl.ds(pl.multiple_of(p * 2 * hidden, 2 * hidden), 2 * hidden)
        left = acts[:, :, at].reshape(tokens, 2 * hidden)

        def step(j, _):
            columns = pl.ds(pl.multiple_of(j * 768, 768), 768)
            result = transposed(left, rows[:, :, columns].reshape(tokens, 768)).astype(bf16)
            for k in range(2):
                for i in range(rows_y):
                    first = k * hidden + i * (hidden // rows_y)
                    part_down[2 * p + k, i, :, columns] = result[
                        first : first + hidden // rows_y
                    ]
            return 0

        lax.fori_loop(0, width // 768, step, 0)
        for k in range(2):
            send_down(2 * p + k).start()
        return 0

    def keep_down(e):
        return pltpu.make_async_copy(
            stage_down.at[lax.rem(e, 2)], down_out.at[e], down_sems.at[lax.rem(e, 2)]
        )

    def finish_down(e, _):
        @pl.when(e >= 2)
        def _():
            keep_down(e - 2).wait()

        send_down(e).wait_recv()
        stage_down[lax.rem(e, 2)] = add(part_down.at[e, y], heard_down.at[e])
        keep_down(e).start()
        return 0

    forward(0)
    z1.wait_recv()
    x1 = row_x(1)
    z2.wait_recv()
    z3 = links.copy(rows.at[2, own], rows.at[3, own], to["z1"])
    x2 = row_x(2)
    load_down.wait()
    combine(0)
    x1.wait_recv()
    c1 = row_c(1)
    c1.wait_recv()
    forward(1)
    z3.wait_recv()
    x3 = row_x(3)
    backward(1)
    sum_c(1)
    x2.wait_recv()
    c2 = row_c(2)
    out_c(0)
    sum_x(1)
    c2.wait_recv()
    forward(2)
    backward(2)
    sum_c(2)
    sum_z(1)
    x3.wait_recv()
    c3 = row_c(3)
    sum_x(2)
    c3.wait_recv()
    forward(3)
    backward(3)
    sum_c(3)
    backward(0)
    sum_x(3)
    sum_c(0)
    sum_z(2)
    for r in range(ZLINE):
        keep_rows(r).wait()
    gathered = (z1, z2, z3, x0, x1, x2, x3, c0, c1, c2, c3)
    for copy in gathered:
        copy.wait_send()
    for r in range(ZLINE):
        fetch_dy(r).start()
    sum_x(0)
    combine(1)
    for r in range(ZLINE):
        fetch_dy(r).wait()
    lax.fori_loop(0, 1, down, 0)
    sum_z(3)
    out_c(1)
    lax.fori_loop(1, 2, down, 0)
    combine(2)
    lax.fori_loop(2, 3, down, 0)
    sum_z(0)
    out_c(2)
    combine(3)
    lax.fori_loop(3, owned // 2, down, 0)
    out_c(3)
    total = parts[0, own].astype(f32)
    for r in (1, 2, 3):
        made["z", r].wait_recv()
        total = total + heard_z[r - 1].astype(f32)
    total_ref[...] = total
    for r in (2, 3):
        keep_combined(r).wait()
        out_x(r)
    lax.fori_loop(0, owned, finish_down, 0)
    for r in range(ZLINE):
        made["ox", r].wait_recv()
    done = gathered + (made["oc", 0], made["oc", 1])
    links.open = [v for v in links.open if not any(v is copy for copy in done)]
    links.close()
    for e in range(owned):
        send_down(e).wait_send()
    for e in (owned - 2, owned - 1):
        keep_down(e).wait()
    for r in (0, ZLINE - 1):
        keep_grads(r).wait()


def moe(rows_y, normed, dy, plain, w_gate_up, w_down, router):
    owned, width, _ = w_gate_up.shape
    hidden = F // ZLINE
    length = normed.shape[0]
    count = dy.shape[1]
    any_space = pl.BlockSpec(memory_space=pl.ANY)
    vmem = pl.BlockSpec(memory_space=pltpu.VMEM)
    sems = pltpu.SemaphoreType.DMA
    span = owned * hidden
    wide = width + 128
    return pl.pallas_call(
        functools.partial(moe_kernel, rows_y),
        name="moe",
        out_shape=(
            jax.ShapeDtypeStruct((ZLINE, count, width), bf16),
            jax.ShapeDtypeStruct((ZLINE, count, 2 * span), bf16),
            jax.ShapeDtypeStruct((owned, hidden // rows_y, width), bf16),
            jax.ShapeDtypeStruct((ZLINE, count // 2, width), bf16),
            jax.ShapeDtypeStruct((ZLINE, length, width), bf16),
            jax.ShapeDtypeStruct((length, wide), f32),
        ),
        in_specs=[vmem, any_space, any_space, any_space, any_space, vmem],
        out_specs=(any_space,) * 5 + (vmem,),
        scratch_shapes=[
            pltpu.VMEM((width, span), bf16),
            pltpu.VMEM((width, span), bf16),
            pltpu.VMEM((owned, hidden, width), bf16),
            pltpu.VMEM((ZLINE, count, width), bf16),
            pltpu.VMEM((ZLINE, count, 128), bf16),
            pltpu.VMEM((2, count, span), bf16),
            pltpu.VMEM((2, count, 2 * span), bf16),
            pltpu.VMEM((ZLINE, count, span), bf16),
            pltpu.VMEM((count, 128), f32),
            pltpu.VMEM((owned, rows_y, hidden // rows_y, width), bf16),
            pltpu.VMEM((owned, hidden // rows_y, width), bf16),
            pltpu.VMEM((2, hidden // rows_y, width), bf16),
            pltpu.VMEM((ZLINE, count, wide), bf16),
            pltpu.VMEM((ZLINE, count // 2, wide), bf16),
            pltpu.VMEM((ZLINE, length, wide), bf16),
            pltpu.VMEM((ZLINE - 1, length, wide), bf16),
            pltpu.VMEM((2, count, width), bf16),
            pltpu.VMEM((ZLINE, count // 2, width), bf16),
            pltpu.VMEM((128, span), bf16),
            sems((MOE_COPIES,)),
            sems((MOE_COPIES,)),
            sems((owned,)),
            sems((owned,)),
            sems((2 * owned + 2,)),
            sems((2,)),
            sems((ZLINE,)),
            sems((ZLINE,)),
            sems((ZLINE,)),
            sems((2,)),
            sems((ZLINE,)),
        ],
        compiler_params=pltpu.CompilerParams(
            collective_id=1, has_side_effects=True, vmem_limit_bytes=63 * 2**20
        ),
    )(normed, dy, plain, w_gate_up, w_down, router)


def finish_kernel(
    rows_y,
    rows_hbm,
    grads_hbm,
    combined_hbm,
    heard_hbm,
    w_output_hbm,
    w_qkv_hbm,
    row_grads,
    gates,
    cotangent,
    residual,
    normed_moe,
    gains,
    router,
    tokens_ref,
    mixed,
    normed,
    queries,
    keys,
    values,
    allowed,
    cosine,
    sine,
    gate_up_out,
    output_out,
    grad_tokens_out,
    out_0,
    out_1,
    out_2,
    rows,
    turned,
    grads,
    part_gate_up,
    heard_gate_up,
    heard_z,
    stage,
    o_own,
    o_x,
    o_z1,
    o_z2,
    w_output,
    w_qkv,
    grad_qkv,
    grad_normed,
    left_output,
    left_qkv,
    right_output,
    right_qkv,
    part_small,
    grad_residual,
    grad_branch,
    base_small,
    *refs,
):
    owned, n = gate_up_out.shape[:2]
    hidden = F // ZLINE
    count, width = rows.shape
    length = tokens_ref.shape[0]
    tokens = ZLINE * count
    dp, ex = lax.axis_index("dp"), lax.axis_index("expert")
    z, y = dp // rows_y, dp % rows_y
    core, side = ex % 2, (ex // 2) % 2
    to = partners(rows_y)
    to["z3"] = (other(to["z1"][0], 2 * rows_y), ex)
    to["xc"] = (dp, other(other(ex, 1), 2))
    z_of = [z, other(z, 1), other(z, 2), other(other(z, 1), 2)]
    half, quarter = n // 2, n // 4
    of_core = pl.ds(pl.multiple_of(core * half, 16), half)
    of_sibling = pl.ds(pl.multiple_of((1 - core) * half, 16), half)
    of_side = pl.ds(pl.multiple_of(side * quarter, 16), quarter)
    of_far_side = pl.ds(pl.multiple_of((1 - side) * quarter, 16), quarter)
    mine = pl.ds(pl.multiple_of(core * half + side * quarter, 16), quarter)
    (
        load_sem,
        own_sems,
        weight_sems,
        grads_sems,
        store_sems,
        y_send,
        y_recv,
        z_send,
        z_recv,
        a_send,
        a_recv,
        f_send,
        f_recv,
        o_send,
        o_recv,
    ) = refs[18:]

    def remote(source, target, send_sem, recv_sem, device):
        return pltpu.make_async_remote_copy(
            src_ref=source,
            dst_ref=target,
            send_sem=send_sem,
            recv_sem=recv_sem,
            device_id=device,
            device_id_type=pl.DeviceIdType.MESH,
        )

    def add(left, right):
        return (left.astype(f32) + right.astype(f32)).astype(bf16)

    def load_rows(r):
        return pltpu.make_async_copy(rows_hbm.at[r], rows, load_sem)

    def load_grads(e, k):
        at = pl.ds(pl.multiple_of((k * owned + e) * hidden, hidden), hidden)
        return pltpu.make_async_copy(
            grads_hbm.at[:, :, at],
            grads.at[lax.rem(e, 2), :, :, pl.ds(k * hidden, hidden)],
            grads_sems.at[lax.rem(e, 2), k],
        )

    load_combined = [
        pltpu.make_async_copy(combined_hbm.at[:, pl.ds(0, length)], o_own, own_sems.at[0]),
        pltpu.make_async_copy(heard_hbm, o_x, own_sems.at[1]),
    ]

    def o_copy(k):
        if k < 2:
            return remote(o_own.at[1 + 2 * k], o_z1.at[k], o_send.at[k], o_recv.at[k], to["z1"])
        return remote(o_own.at[2], o_z2, o_send.at[k], o_recv.at[k], to["z2"])

    def o_start():
        for load in load_combined:
            load.wait()
        for r in (3, 1, 2, 0):
            o_own[r] = add(o_own[r], o_x[r])
            if r % 2:
                o_copy(r // 2).start()

    def o_after_z1():
        for k in (1, 0):
            o_copy(k).wait_recv()
            o_own[2 * k] = add(o_own[2 * k], o_z1[k])
            if k:
                o_copy(2).start()

    def o_end():
        o_copy(2).wait_recv()
        total = o_own[0].astype(f32) + o_z2[...].astype(f32)
        output_out[...] = (residual[...] + total).astype(bf16)

    def left_copies(k, source, target):
        made = []
        for m, name in ((1, "c"), (2, "x"), (3, "xc")):
            c = 1 - core if m % 2 else core
            s = 1 - side if m // 2 else side
            made.append(
                remote(
                    source.at[:, c, s],
                    target.at[:, :, pl.ds(m * length, length)],
                    f_send.at[k, m],
                    f_recv.at[k, m],
                    to[name],
                )
            )
        return made

    def right_copy(k, source, target, m):
        if m == 3:
            source = target.at[pl.ds(2 * length, length)]
        return remote(
            source,
            target.at[pl.ds(m * length, length)],
            f_send.at[k, m],
            f_recv.at[k, m],
            to["x" if m == 2 else "c"],
        )

    class Sum:
        def __init__(self, k, out, rows):
            self.k, self.out, self.rows = k, out, rows
            self.own, self.c, self.x, self.y, self.z1, self.z2 = refs[6 * k : 6 * k + 6]

        def copy(self, step, source, target, device):
            return remote(
                source, target, a_send.at[self.k, step], a_recv.at[self.k, step], device
            )

        def to_y(self, b):
            return self.copy(8 + b, self.own.at[b, 1 - y, self.rows], self.y.at[b], to["y"])

        def to_z1(self, m):
            return self.copy(
                1 + m, self.own.at[z_of[1 + 2 * m], y, self.rows], self.z1.at[m], to["z1"]
            )

        def to_z2(self):
            return self.copy(3, self.own.at[z_of[2], y, self.rows], self.z2, to["z2"])

        def back_x(self):
            return self.copy(4, self.out.at[mine], self.out.at[mine], to["x"])

        def back_c(self):
            return self.copy(5, self.out.at[of_core], self.out.at[of_core], to["c"])

        def to_c(self):
            return self.copy(6, part_small.at[:, :, of_sibling], self.c, to["c"])

        def to_x(self):
            return self.copy(7, self.own.at[:, :, of_far_side], self.x, to["x"])

        def after_c(self):
            self.to_c().wait_recv()
            for b in range(ZLINE):
                for k in range(rows_y):
                    self.own[b, k] = add(part_small[b, k, of_core], self.c[b, k])
            self.to_x().start()

        def after_x(self):
            self.to_x().wait_recv()
            for b in range(ZLINE):
                for k in range(rows_y):
                    self.own[b, k, self.rows] = add(self.own[b, k, self.rows], self.x[b, k])
            self.along_y()

        def along_y(self):
            for b in range(ZLINE):
                self.to_y(b).start()

        def after_y(self):
            for b in range(ZLINE):
                self.to_y(b).wait_recv()
                self.own[b, y, self.rows] = add(self.own[b, y, self.rows], self.y[b])
            for m in (1, 0):
                self.to_z1(m).start()

        def after_z1(self):
            for m in (1, 0):
                self.to_z1(m).wait_recv()
                at = z_of[2 * m]
                self.own[at, y, self.rows] = add(self.own[at, y, self.rows], self.z1[m])
                if m:
                    self.to_z2().start()

        def after_z2(self):
            self.to_z2().wait_recv()
            self.out[mine] = add(self.own[z, y, self.rows], self.z2[...])
            self.back_x().start()

        def after_back(self):
            self.back_x().wait_recv()
            self.back_c().start()

        def close(self):
            self.back_c().wait()
            for made in (self.to_z1(0), self.to_z1(1), self.to_z2(), self.back_x()):
                made.wait_send()
            for b in range(ZLINE):
                self.to_y(b).wait_send()

    whole = pl.ds(0, quarter)
    output = Sum(0, out_0, whole)
    small = Sum(1, out_1, of_side)
    qkv = Sum(2, out_2, whole)

    def products(array, left, right):
        rows_all = left[...].reshape(ZLINE * rows_y * quarter, 4 * length)

        def step(j, _):
            at = pl.ds(pl.multiple_of(j * 512, 512), 512)
            result = jnp.dot(rows_all, right[:, at], preferred_element_type=f32).astype(bf16)
            array.own[:, :, :, at] = result.reshape(ZLINE, rows_y, quarter, 512)
            return 0

        lax.fori_loop(0, right.shape[1] // 512, step, 0)
        array.along_y()

    def load_output(i):
        step = w_output.shape[1]
        at = pl.ds(pl.multiple_of(i * step, step), step)
        return pltpu.make_async_copy(
            w_output_hbm.at[at], w_output.at[lax.rem(i, 2)], weight_sems.at[0, lax.rem(i, 2)]
        )

    def load_qkv(i):
        step = w_qkv.shape[1]
        at = pl.ds(pl.multiple_of(i * step, step), step)
        return pltpu.make_async_copy(
            w_qkv_hbm.at[at], w_qkv.at[lax.rem(i, 2)], weight_sems.at[1, lax.rem(i, 2)]
        )

    def unrotate(value):
        lanes = value.shape[1]
        lane = lax.broadcasted_iota(jnp.int32, value.shape, 1)
        swapped = jnp.where(
            lane % HD < HD // 2,
            pltpu.roll(value, lanes - HD // 2, 1),
            pltpu.roll(value, HD // 2, 1),
        )
        return (value * cosine[:, :lanes] + swapped * sine[:, :lanes]).astype(bf16)

    per_group = H // KV
    wide = GROUP * per_group * HD
    narrow = GROUP * HD

    def attend(i, _):
        load_output(i).wait()
        at = pl.ds(pl.multiple_of(i * wide, wide), wide)
        kv_at = pl.ds(pl.multiple_of(i * narrow, narrow), narrow)
        grad_mixed = against(grad_branch[...], w_output[lax.rem(i, 2)]).astype(bf16)
        query, key, value = queries[:, at], keys[:, kv_at], values[:, kv_at]
        is_allowed = allowed[...] > 0.5
        grad_queries, grad_keys, grad_values = [], [], []
        for k in range(GROUP):
            k_head, v_head = key[:, k * HD : (k + 1) * HD], value[:, k * HD : (k + 1) * HD]
            grad_k = grad_v = None
            for j in range(k * per_group, (k + 1) * per_group):
                q_head = query[:, j * HD : (j + 1) * HD]
                mixed_head = grad_mixed[:, j * HD : (j + 1) * HD]
                scores = jnp.where(is_allowed, against(q_head, k_head) * 0.125, -1e30)
                lifted = jnp.exp(scores - jnp.max(scores, axis=-1, keepdims=True))
                weights = lifted / jnp.sum(lifted, axis=-1, keepdims=True)
                grad_weights = against(mixed_head, v_head)
                inner = jnp.sum(weights * grad_weights, axis=-1, keepdims=True)
                grad_scores = (weights * (grad_weights - inner)).astype(bf16)
                part_v = transposed(weights.astype(bf16), mixed_head)
                part_k = transposed(grad_scores, q_head)
                grad_v = part_v if grad_v is None else grad_v + part_v
                grad_k = part_k if grad_k is None else grad_k + part_k
                grad_queries.append(
                    jnp.dot(grad_scores, k_head, preferred_element_type=f32) * 0.125
                )
            grad_keys.append(grad_k * 0.125)
            grad_values.append(grad_v)
        grad_qkv[:, at] = unrotate(jnp.concatenate(grad_queries, axis=1))
        k_at = pl.ds(pl.multiple_of(H * HD + i * narrow, narrow), narrow)
        v_at = pl.ds(pl.multiple_of((H + KV) * HD + i * narrow, narrow), narrow)
        grad_qkv[:, k_at] = unrotate(jnp.concatenate(grad_keys, axis=1))
        grad_qkv[:, v_at] = jnp.concatenate(grad_values, axis=1).astype(bf16)

        @pl.when(i + 2 < KV // GROUP)
        def _():
            load_output(i + 2).start()

        return 0

    def column(value, lane):
        at_lane = lax.broadcasted_iota(jnp.int32, (length, 128), 1) == lane
        at_lane = at_lane.astype(f32).astype(bf16)
        high = value.astype(bf16)
        low = (value - high.astype(f32)).astype(bf16)
        return transposed(high, at_lane) + transposed(low, at_lane)

    def norm_grads():
        grad_gates = row_grads[:, width:]
        inner = jnp.sum(gates[...] * grad_gates, axis=-1, keepdims=True)
        grad_logits = (gates[...] * (grad_gates - inner)).astype(bf16)
        grad_normed_moe = row_grads[:, :width] + against(grad_logits, router[...])
        inv = lax.rsqrt(jnp.mean(residual[...] * residual[...], axis=-1, keepdims=True) + epsilon)
        unit = residual[...] * inv
        scaled = grad_normed_moe * gains[1:2]
        total = cotangent[...].astype(f32) + inv * (
            scaled - unit * jnp.mean(scaled * unit, axis=-1, keepdims=True)
        )
        grad_residual[...] = total
        grad_branch[...] = total.astype(bf16)
        base_small[...] = transposed(normed_moe[...], grad_logits) + column(
            grad_normed_moe * unit, EXPERTS + 1
        )

    def input_grads():
        tile = w_qkv.shape[1]

        def step(i, _):
            load_qkv(i).wait()
            at = pl.ds(pl.multiple_of(i * tile, tile), tile)
            grad_normed[:, at] = against(grad_qkv[...], w_qkv[lax.rem(i, 2)])

            @pl.when(i + 2 < width // tile)
            def _():
                load_qkv(i + 2).start()

            return 0

        lax.fori_loop(0, width // tile, step, 0)
        inputs = tokens_ref[...].astype(f32)
        inv = lax.rsqrt(jnp.mean(inputs * inputs, axis=-1, keepdims=True) + epsilon)
        unit = inputs * inv
        onto = grad_normed[...] * unit
        scaled = grad_normed[...] * gains[:1]
        grad_tokens_out[...] = (
            grad_residual[...]
            + inv * (scaled - unit * jnp.mean(scaled * unit, axis=-1, keepdims=True))
        ).astype(bf16)
        part = base_small[...] + column(onto, EXPERTS)
        part_small[...] = part.astype(bf16).reshape(part_small.shape)
        small.to_c().start()

    load_rows(0).start()
    for load in load_combined:
        load.start()
    for e in range(2):
        for k in range(2):
            load_grads(e, k).start()
    for i in range(2):
        load_output(i).start()
        load_qkv(i).start()
    norm_grads()
    greet([to[name] for name in ("z1", "z2", "z3", "y", "x", "c", "xc")])
    own_tokens = pl.ds(0, length)
    lefts = left_copies(0, mixed, left_output) + left_copies(1, normed, left_qkv)
    rights = {m: right_copy(2, grad_branch, right_output, m) for m in (1, 2, 3)}
    qkv_rights = {m: right_copy(3, grad_qkv, right_qkv, m) for m in (1, 2, 3)}
    rights[2].start()
    rights[1].start()
    for made in lefts:
        made.start()
    left_output[:, :, own_tokens] = mixed[:, core, side]
    left_qkv[:, :, own_tokens] = normed[:, core, side]
    right_output[own_tokens] = grad_branch[...]
    o_start()

    for r in range(ZLINE):
        load_rows(r).wait()

        def turn(j, _, r=r):
            at = pl.ds(pl.multiple_of(j * 256, 256), 256)
            turned[at, pl.ds(r * count, count)] = rows[:, at].T
            return 0

        lax.fori_loop(0, width // 256, turn, 0)
        if r + 1 < ZLINE:
            load_rows(r + 1).start()

    def send_y(e):
        return remote(
            part_gate_up.at[e, 1 - y], heard_gate_up.at[e], y_send.at[e], y_recv.at[e], to["y"]
        )

    def send_z(e, m):
        return remote(
            part_gate_up.at[e, y, z_of[m]],
            heard_z.at[m - 1, e],
            z_send.at[m - 1, e],
            z_recv.at[m - 1, e],
            to[f"z{m}"],
        )

    def reduce(e):
        send_y(e).wait_recv()
        for b in range(ZLINE):
            part_gate_up[e, y, b] = add(part_gate_up[e, y, b], heard_gate_up[e, b])
        for m in range(1, ZLINE):
            send_z(e, m).start()

    def gate_up(e, _):
        for k in range(2):
            load_grads(e, k).wait()
        right = grads[lax.rem(e, 2)].reshape(tokens, 2 * hidden)

        def step(b, _):
            at = pl.ds(pl.multiple_of(b * rows_y * n, 128), rows_y * n)
            result = jnp.dot(turned[at, :], right, preferred_element_type=f32).astype(bf16)
            for k in range(rows_y):
                part_gate_up[e, k, b] = result[k * n : (k + 1) * n]
            return 0

        lax.fori_loop(0, ZLINE, step, 0)

        @pl.when(e + 2 < owned)
        def _():
            for k in range(2):
                load_grads(e + 2, k).start()

        return 0

    lax.fori_loop(0, 1, gate_up, 0)
    send_y(0).start()
    lax.fori_loop(1, 2, gate_up, 0)
    send_y(1).start()
    rights[2].wait_recv()
    rights[3].start()
    o_after_z1()
    for made in lefts:
        made.wait_recv()
    rights[1].wait_recv()
    rights[3].wait_recv()
    products(output, left_output, right_output)
    lax.fori_loop(0, KV // GROUP // 2, attend, 0)
    lax.fori_loop(2, 3, gate_up, 0)
    send_y(2).start()
    reduce(0)
    lax.fori_loop(KV // GROUP // 2, KV // GROUP, attend, 0)
    qkv_rights[2].start()
    qkv_rights[1].start()
    o_end()
    right_qkv[own_tokens] = grad_qkv[...]
    lax.fori_loop(3, 4, gate_up, 0)
    send_y(3).start()
    reduce(1)
    output.after_y()
    input_grads()
    lax.fori_loop(4, 5, gate_up, 0)
    send_y(4).start()
    qkv_rights[2].wait_recv()
    qkv_rights[3].start()
    reduce(2)
    qkv_rights[1].wait_recv()
    qkv_rights[3].wait_recv()
    products(qkv, left_qkv, right_qkv)
    small.after_c()
    reduce(3)
    output.after_z1()
    lax.fori_loop(5, 7, gate_up, 0)
    send_y(5).start()
    output.after_z2()
    lax.fori_loop(7, owned, gate_up, 0)
    small.after_x()
    reduce(4)
    send_y(6).start()
    qkv.after_y()
    send_y(7).start()
    output.after_back()
    reduce(5)
    send_y(8).start()
    small.after_y()
    reduce(6)
    send_y(9).start()
    qkv.after_z1()
    reduce(7)
    small.after_z1()
    qkv.after_z2()
    reduce(8)
    small.after_z2()
    qkv.after_back()
    small.after_back()
    reduce(9)

    def keep(e):
        return pltpu.make_async_copy(
            stage.at[lax.rem(e, 2)], gate_up_out.at[e], store_sems.at[lax.rem(e, 2)]
        )

    def collect(e, _):
        slot = lax.rem(e, 2)

        @pl.when(e >= 2)
        def _():
            keep(e - 2).wait()

        for m in range(ZLINE):
            if m:
                send_z(e, m).wait_recv()
                block = heard_z[m - 1, e]
            else:
                block = part_gate_up[e, y, z]
            for k in range(2):
                at = pl.ds(pl.multiple_of(k * F + z_of[m] * hidden, hidden), hidden)
                stage[slot, :, at] = block[:, k * hidden : (k + 1) * hidden]
        keep(e).start()
        return 0

    lax.fori_loop(0, owned, collect, 0)

    for e in (owned - 2, owned - 1):
        keep(e).wait()

    def close(e, _):
        send_y(e).wait_send()
        for m in range(1, ZLINE):
            send_z(e, m).wait_send()
        return 0

    lax.fori_loop(0, owned, close, 0)
    for array in (output, small, qkv):
        array.close()
    small.to_c().wait_send()
    small.to_x().wait_send()
    for k in range(3):
        o_copy(k).wait_send()
    for made in lefts + list(rights.values()) + list(qkv_rights.values()):
        made.wait_send()


def finish(rows_y, rows, grads, combined, heard, w_output, w_qkv, *small):
    _, count, width = rows.shape
    hidden = F // ZLINE
    owned = grads.shape[2] // (2 * hidden)
    length = small[0].shape[0]
    blocks = ZLINE * rows_y
    n = width // blocks
    columns = (w_output.shape[1], 128, w_qkv.shape[1])
    any_space = pl.BlockSpec(memory_space=pl.ANY)
    vmem = pl.BlockSpec(memory_space=pltpu.VMEM)
    sems = pltpu.SemaphoreType.DMA

    def summed(wide, own_rows):
        heard = own_rows != n // 4
        return [
            pltpu.VMEM((ZLINE, rows_y, own_rows, wide), bf16),
            pltpu.VMEM((ZLINE, rows_y, n // 2, wide) if heard else (16, 128), bf16),
            pltpu.VMEM((ZLINE, rows_y, n // 4, wide) if heard else (16, 128), bf16),
            pltpu.VMEM((ZLINE, n // 4, wide), bf16),
            pltpu.VMEM((2, n // 4, wide), bf16),
            pltpu.VMEM((n // 4, wide), bf16),
        ]

    return pl.pallas_call(
        functools.partial(finish_kernel, rows_y),
        name="finish",
        out_shape=(
            jax.ShapeDtypeStruct((owned, n, 2 * F), bf16),
            jax.ShapeDtypeStruct((length, width), bf16),
            jax.ShapeDtypeStruct((length, width), bf16),
        )
        + tuple(jax.ShapeDtypeStruct((n, v), bf16) for v in columns),
        in_specs=[any_space] * 6 + [vmem] * len(small),
        out_specs=(any_space,) + (vmem,) * 5,
        scratch_shapes=[
            pltpu.VMEM((count, width), bf16),
            pltpu.VMEM((width, ZLINE * count), bf16),
            pltpu.VMEM((2, ZLINE, count, 2 * hidden), bf16),
            pltpu.VMEM((owned, rows_y, ZLINE, n, 2 * hidden), bf16),
            pltpu.VMEM((owned, ZLINE, n, 2 * hidden), bf16),
            pltpu.VMEM((ZLINE - 1, owned, n, 2 * hidden), bf16),
            pltpu.VMEM((2, n, 2 * F), bf16),
            pltpu.VMEM((ZLINE, length, width), bf16),
            pltpu.VMEM((ZLINE, length, width), bf16),
            pltpu.VMEM((2, length, width), bf16),
            pltpu.VMEM((length, width), bf16),
            pltpu.VMEM((2, GROUP * (H // KV) * HD, width), bf16),
            pltpu.VMEM((2, 256, columns[2]), bf16),
            pltpu.VMEM((length, columns[2]), bf16),
            pltpu.VMEM((length, width), f32),
            pltpu.VMEM((blocks, n // 4, 4 * length), bf16),
            pltpu.VMEM((blocks, n // 4, 4 * length), bf16),
            pltpu.VMEM((4 * length, columns[0]), bf16),
            pltpu.VMEM((4 * length, columns[2]), bf16),
            pltpu.VMEM((ZLINE, rows_y, n, 128), bf16),
            pltpu.VMEM((length, width), f32),
            pltpu.VMEM((length, width), bf16),
            pltpu.VMEM((width, 128), f32),
            *summed(columns[0], n // 4),
            *summed(columns[1], n // 2),
            *summed(columns[2], n // 4),
            sems,
            sems((2,)),
            sems((2, 2)),
            sems((2, 2)),
            sems((2,)),
            sems((owned,)),
            sems((owned,)),
            sems((ZLINE - 1, owned)),
            sems((ZLINE - 1, owned)),
            sems((3, 8 + ZLINE)),
            sems((3, 8 + ZLINE)),
            sems((4, 4)),
            sems((4, 4)),
            sems((3,)),
            sems((3,)),
        ],
        compiler_params=pltpu.CompilerParams(
            collective_id=3, has_side_effects=True, vmem_limit_bytes=63 * 2**20
        ),
    )(rows, grads, combined, heard, w_output, w_qkv, *small)


def permuted(
    tokens,
    segments,
    routes,
    w_query,
    w_key,
    w_value,
    w_output,
    w_router,
    gain_attn,
    gain_moe,
    w_gate_up,
    w_down,
    cotangent,
):
    place = Place()
    length, width = tokens.shape
    owned = w_gate_up.shape[0]
    rows = w_query.shape[0]
    hidden = F // ZLINE
    per_group = H // KV
    q_end, k_end, v_end = H * HD, (H + KV) * HD, (H + 2 * KV) * HD
    o_end = v_end + width

    small = jnp.concatenate(
        [w_router, gain_attn[:, None], gain_moe[:, None], jnp.zeros((rows, 128 - EXPERTS - 2), bf16)],
        axis=1,
    )
    shard = jnp.concatenate([w_query, w_key, w_value, w_output, small], axis=1)
    full, order = gather_weights(place, shard)
    full_qkv, full_output = full[:, :v_end], full[:, v_end:o_end]
    full_small = transposed(order, full[:, o_end:]).astype(bf16)
    full_router = full_small[:, :EXPERTS]
    attn_gain = full_small[:, EXPERTS].astype(f32)
    moe_gain = full_small[:, EXPERTS + 1].astype(f32)

    chosen_mask = jnp.any(
        routes[:, :, None] == jnp.arange(EXPERTS, dtype=jnp.int32), axis=1
    )
    dy_block = jnp.concatenate(
        [cotangent, chosen_mask.astype(bf16), jnp.zeros((length, 128 - EXPERTS), bf16)], axis=1
    )
    dy_groups = gather_tokens(place, dy_block)

    cosine_table, sine_table = tables(length, HD)
    inputs = tokens.astype(f32)
    inv_attn = lax.rsqrt(jnp.mean(inputs * inputs, axis=-1, keepdims=True) + epsilon)
    unit_attn = inputs * inv_attn
    normed = (unit_attn * attn_gain).astype(bf16)
    normed = against(normed, order).astype(bf16)
    qkv = dot(normed, full_qkv)
    queries = rotate(qkv[:, :q_end].reshape(length, H, HD), cosine_table, sine_table)
    queries = queries.astype(bf16).reshape(length, KV, per_group, HD)
    key_rows = rotate(
        qkv[:, q_end:k_end].reshape(length, KV, HD), cosine_table, sine_table
    ).astype(bf16)
    values = qkv[:, k_end:].astype(bf16).reshape(length, KV, HD)
    segment = segments[0]
    position = jnp.arange(length, dtype=jnp.int32)
    allowed = (segment[:, None] == segment[None, :]) & (position[:, None] >= position[None, :])
    scores = (
        jnp.einsum("qkgd,skd->kgqs", queries, key_rows, preferred_element_type=f32) * 0.125
    )
    scores = jnp.where(allowed, scores, -1e30)
    maximum = jnp.max(scores, axis=-1, keepdims=True)
    lifted_scores = jnp.exp(scores - maximum)
    full_weights = lifted_scores / jnp.sum(lifted_scores, axis=-1, keepdims=True)
    attn_weights = full_weights.astype(bf16)
    mixed = jnp.einsum("kgqs,skd->qkgd", attn_weights, values, preferred_element_type=f32)
    mixed = mixed.reshape(length, H * HD).astype(bf16)
    mixed = against(mixed, order).astype(bf16)
    residual = inputs + dot(mixed, full_output)
    inv_moe = lax.rsqrt(jnp.mean(residual * residual, axis=-1, keepdims=True) + epsilon)
    unit_moe = residual * inv_moe
    normed_moe = (unit_moe * moe_gain).astype(bf16)

    def gates_of(rows_in, mask):
        logits = jnp.where(mask, dot(rows_in, full_router), -1e30)
        lifted = jnp.where(mask, jnp.exp(logits - jnp.max(logits, axis=-1, keepdims=True)), 0.0)
        return lifted / jnp.sum(lifted, axis=-1, keepdims=True)

    gates = gates_of(normed_moe, chosen_mask)

    def columns(start):
        cut = lax.dynamic_slice_in_dim(w_gate_up, start + place.z * hidden, hidden, 2)
        return cut.swapaxes(0, 1).reshape(width, owned * hidden)

    slice_gate_up = jnp.concatenate([columns(0), columns(F)], axis=1)
    slice_down = lax.dynamic_slice_in_dim(w_down, place.z * hidden, hidden, 1)
    slice_down = slice_down.reshape(owned * hidden, width)
    moe_groups = gather_tokens(place, normed_moe)
    span = owned * hidden
    acts, grads_gate_up, gate_parts = [], [], []
    for normed_rows, dy_rows in zip(moe_groups, dy_groups):
        count = normed_rows.shape[0]
        group_gates = gates_of(normed_rows, dy_rows[:, width : width + EXPERTS] > 0.5)
        group_gates = lax.dynamic_slice_in_dim(group_gates, place.ex * owned, owned, 1)
        spread_gates = jnp.broadcast_to(group_gates[:, :, None], (count, owned, hidden))
        spread_gates = spread_gates.reshape(count, span)
        gate_up = dot(normed_rows, slice_gate_up)
        gate_part, up_part = gate_up[:, :span], gate_up[:, span:]
        plain_grad = against(dy_rows[:, :width], slice_down)
        sigmoid_gate = jax.nn.sigmoid(gate_part)
        swished = gate_part * sigmoid_gate
        activation = swished * up_part
        grad_act = plain_grad * spread_gates
        gate_parts.append(jnp.sum((plain_grad * activation).reshape(count, owned, hidden), axis=-1))
        acts.append((spread_gates * activation).astype(bf16))
        grads_gate_up.append(
            jnp.concatenate(
                [
                    grad_act * up_part * sigmoid_gate * (1.0 + gate_part * (1.0 - sigmoid_gate)),
                    grad_act * swished,
                ],
                axis=-1,
            ).astype(bf16)
        )
    row_parts = [against(g, slice_gate_up).astype(bf16) for g in grads_gate_up]
    row_grads = scatter_tokens(place, row_parts, length)
    out_parts = [dot(a, slice_down).astype(bf16) for a in acts]
    output = (residual + scatter_tokens(place, out_parts, length)).astype(bf16)

    gate_parts = [g.T for g in gate_parts]
    two = [gate_parts[i] + swap(gate_parts[i + 2], "dp", place.z_bits[1]) for i in range(2)]
    mine = two[0] + swap(two[1], "dp", place.z_bits[0])
    mine = mine.reshape(owned, 2, place.ex_size // 2, length)
    heard = [
        swap(mine[:, m % 2, m // 2], "expert", m) if m else mine[:, 0, 0]
        for m in range(place.ex_size)
    ]
    heard = jnp.stack(heard)
    grad_gates = jnp.concatenate(
        [pick(heard, place.ex ^ j) for j in range(place.ex_size)], axis=0
    ).T
    grad_logits = (
        gates * (grad_gates - jnp.sum(gates * grad_gates, axis=-1, keepdims=True))
    ).astype(bf16)

    all_rows = jnp.concatenate([v for v in moe_groups], axis=0)
    all_dy = jnp.concatenate([v[:, :width] for v in dy_groups], axis=0)
    all_grads = jnp.concatenate(grads_gate_up, axis=0)
    all_acts = jnp.concatenate(acts, axis=0)

    def reduce_y(part, axis):
        part = jnp.moveaxis(part, axis, 0)
        for mask in place.y_bits[::-1]:
            at = (place.y // mask) % 2
            half = part.reshape((2, part.shape[0] // 2) + part.shape[1:])
            away = swap(pick(half, 1 - at), "dp", mask)
            part = (pick(half, at).astype(f32) + away.astype(f32)).astype(bf16)
        return part[0]

    shard_down = transposed(all_acts, all_dy).astype(bf16)
    shard_down = shard_down.reshape(owned, place.rows_y, hidden // place.rows_y, width)
    shard_down = reduce_y(shard_down, 1).astype(f32)
    part_gate_up = transposed(all_rows, all_grads).astype(bf16)
    part_gate_up = part_gate_up.reshape(ZLINE, place.rows_y, rows, 2 * span)
    part_gate_up = reduce_y(part_gate_up, 1)
    heard = [pick(part_gate_up, place.z)] + [
        swap(pick(part_gate_up, place.z ^ m), "dp", m * place.rows_y) for m in range(1, ZLINE)
    ]
    heard = jnp.stack(heard)
    shard_gate_up = jnp.stack([pick(heard, place.z ^ j) for j in range(ZLINE)], axis=0)
    shard_gate_up = shard_gate_up.reshape(ZLINE, rows, 2, owned, hidden)
    shard_gate_up = shard_gate_up.transpose(3, 1, 2, 0, 4).reshape(owned, rows, 2 * F).astype(f32)

    grad_out = cotangent.astype(f32)
    part_router = transposed(normed_moe, grad_logits)
    grad_normed_moe = row_grads + against(grad_logits, full_router)
    part_gain_moe = jnp.sum(grad_normed_moe * unit_moe, axis=0)
    scaled_moe = grad_normed_moe * moe_gain
    grad_residual = grad_out + inv_moe * (
        scaled_moe - unit_moe * jnp.mean(scaled_moe * unit_moe, axis=-1, keepdims=True)
    )
    grad_branch = grad_residual.astype(bf16)
    part_output = transposed(mixed, grad_branch)
    grad_mixed = dot(against(grad_branch, full_output).astype(bf16), order).astype(bf16)
    grad_mixed = grad_mixed.reshape(length, KV, per_group, HD)
    grad_weights = jnp.einsum(
        "qkgd,skd->kgqs", grad_mixed, values, preferred_element_type=f32
    )
    grad_values = jnp.einsum(
        "kgqs,qkgd->skd", attn_weights, grad_mixed, preferred_element_type=f32
    )
    grad_values = grad_values.astype(bf16).reshape(length, KV * HD)
    grad_scores = (
        full_weights * (grad_weights - jnp.sum(full_weights * grad_weights, axis=-1, keepdims=True))
    ).astype(bf16)
    grad_queries = (
        jnp.einsum("kgqs,skd->qkgd", grad_scores, key_rows, preferred_element_type=f32) * 0.125
    )
    grad_queries = rotate(grad_queries.reshape(length, H, HD), cosine_table, -sine_table)
    grad_queries = grad_queries.astype(bf16).reshape(length, H * HD)
    grad_keys = (
        jnp.einsum("kgqs,qkgd->skd", grad_scores, queries, preferred_element_type=f32) * 0.125
    )
    grad_keys = rotate(grad_keys, cosine_table, -sine_table)
    grad_keys = grad_keys.astype(bf16).reshape(length, KV * HD)
    grad_qkv = jnp.concatenate([grad_queries, grad_keys, grad_values], axis=1)
    part_qkv = transposed(normed, grad_qkv)
    grad_normed = against(grad_qkv, full_qkv)
    grad_normed = lax.dot_general(
        grad_normed,
        order.astype(f32),
        (((1,), (0,)), ((), ())),
        precision=lax.Precision.HIGHEST,
        preferred_element_type=f32,
    )
    part_gain_attn = jnp.sum(grad_normed * unit_attn, axis=0)
    scaled_attn = grad_normed * attn_gain
    grad_tokens = (
        grad_residual
        + inv_attn
        * (scaled_attn - unit_attn * jnp.mean(scaled_attn * unit_attn, axis=-1, keepdims=True))
    ).astype(bf16)
    part_small = jnp.concatenate(
        [
            part_router.astype(bf16),
            part_gain_attn[:, None].astype(bf16),
            part_gain_moe[:, None].astype(bf16),
            jnp.zeros((width, 128 - EXPERTS - 2), bf16),
        ],
        axis=1,
    )
    part_small = dot(order, part_small).astype(bf16)
    summed = scatter_weights(
        place,
        jnp.concatenate([part_qkv.astype(bf16), part_output.astype(bf16), part_small], axis=1),
    )
    return (
        output,
        grad_tokens,
        summed[:, :q_end],
        summed[:, q_end:k_end],
        summed[:, k_end:v_end],
        summed[:, v_end:o_end],
        summed[:, o_end : o_end + EXPERTS],
        summed[:, o_end + EXPERTS],
        summed[:, o_end + EXPERTS + 1],
        shard_gate_up,
        shard_down,
    )


def local(
    tokens,
    segments,
    routes,
    w_query,
    w_key,
    w_value,
    w_output,
    w_router,
    gain_attn,
    gain_moe,
    w_gate_up,
    w_down,
    cotangent,
):
    place = Place()
    if place.ex_size != 4 or place.rows_y != 2:
        return permuted(
            tokens,
            segments,
            routes,
            w_query,
            w_key,
            w_value,
            w_output,
            w_router,
            gain_attn,
            gain_moe,
            w_gate_up,
            w_down,
            cotangent,
        )
    length, width = tokens.shape
    per_group = H // KV
    q_end, k_end, v_end = H * HD, (H + KV) * HD, (H + 2 * KV) * HD

    angles = np.arange(length)[:, None] * 10000.0 ** (-2.0 * np.arange(HD // 2) / HD)[None, :]
    repeats = (1, GROUP * per_group)
    cosine = jnp.asarray(np.tile(np.tile(np.cos(angles), (1, 2)), repeats), f32)
    sine = np.concatenate([np.sin(angles), -np.sin(angles)], axis=1)
    sine = jnp.asarray(np.tile(sine, repeats), f32)
    (
        full_qkv,
        full_output,
        all_dy,
        plain_grads,
        full_small,
        queries,
        key_rows,
        values,
        residual,
        normed_moe,
        normed,
        mixed,
        gains,
        gates,
        allowed,
    ) = gather(
        place.rows_y,
        (w_query, w_key, w_value, w_output, w_router, gain_attn[None, :], gain_moe[None, :]),
        cotangent,
        tokens,
        segments,
        routes,
        cosine,
        sine,
        w_down,
    )
    full_small = full_small.reshape(width, 128)
    all_rows, all_grads, shard_down, combined, heard, row_grads = moe(
        place.rows_y, normed_moe, all_dy, plain_grads, w_gate_up, w_down, full_small
    )
    shard_gate_up, output, grad_tokens, sum_output, sum_small, sum_qkv = finish(
        place.rows_y,
        all_rows,
        all_grads,
        combined,
        heard,
        full_output.reshape(width, width),
        full_qkv.reshape(width, v_end),
        row_grads,
        gates,
        cotangent,
        residual,
        normed_moe,
        gains,
        full_small,
        tokens,
        mixed,
        normed,
        queries,
        key_rows,
        values,
        allowed,
        cosine,
        sine,
    )
    return (
        output,
        grad_tokens,
        sum_qkv[:, :q_end].astype(f32),
        sum_qkv[:, q_end:k_end].astype(f32),
        sum_qkv[:, k_end:].astype(f32),
        sum_output.astype(f32),
        sum_small[:, :EXPERTS].astype(f32),
        sum_small[:, EXPERTS].astype(f32),
        sum_small[:, EXPERTS + 1].astype(f32),
        shard_gate_up.astype(f32),
        shard_down.astype(f32),
    )


def solution(mesh):
    return jax.shard_map(
        local,
        mesh=mesh,
        in_specs=(
            P(("dp", "expert"), None),
            P(("dp", "expert"), None),
            P(("dp", "expert"), None),
            P("dp", None),
            P("dp", None),
            P("dp", None),
            P("dp", None),
            P("dp", None),
            P("dp"),
            P("dp"),
            P("expert", None, None),
            P("expert", None, None),
            P(("dp", "expert"), None),
        ),
        out_specs=(
            P(("dp", "expert"), None),
            P(("dp", "expert"), None),
            P("dp", None),
            P("dp", None),
            P("dp", None),
            P("dp", None),
            P("dp", None),
            P("dp"),
            P("dp"),
            P("expert", "dp", None),
            P("expert", "dp", None),
        ),
        check_vma=False,
    )
```

profile of v0, /device:TPU:0, one launch (start us, length us, event | category | flops | bytes accessed | tf_op | source)
XLA Modules:
  0.0 441.8 jit_solution(2169203770384122100)
XLA Ops:
  0.6 1.2 broadcast_in_dim.6.gain_attn
  1.9 1.2 broadcast_in_dim.7.gain_moe
  3.1 1.4 copy.29.w_router
  4.5 1.4 copy.30.routes
  5.9 107.3 %gather.1 = (bf16[8,192,2560]{2,1,0:T(8,128)(2,1)}, bf16[8,192,1536]{2,1,0:T(8,128)(2,1)}, bf16[4,512,1664]{2,1,0:T(8,128)(2,1)}, bf16[4,512,1280]{2,1,0:T(8,128...) custom-call(bf16[192,1536]{1,0:T(8,128)(2,1)} %w_query.1, ...), custom_call_target="tpu_custom_call" | custom-call | tf_op jit(solution)/shard_map/gather/pallas_call | solution.py:626
  113.3 142.2 %moe.1 = (bf16[4,512,1536]{2,1,0:T(8,128)(2,1)}, bf16[4,512,2560]{2,1,0:T(8,128)(2,1)}, bf16[10,64,1536]{2,1,0:T(8,128)(2,1)}, bf16[4,256,1536]{2,1,0:T(8,128)(2...) custom-call(bf16[128,1536]{1,0:T(8,128)(2,1)} %get-tuple-element.38.normed_ref.normed_moe, ...), custom_call_target="tpu_custom_call" | custom-call | tf_op jit(solution)/shard_map/moe/pallas_call | solution.py:1049
  255.5 168.2 %finish.1 = (bf16[10,192,1024]{2,1,0:T(8,128)(2,1)}, bf16[128,1536]{1,0:T(8,128)(2,1)}, bf16[128,1536]{1,0:T(8,128)(2,1)}, bf16[192,1536]{1,0:T(8,128)(2,1)}, bf...) custom-call(bf16[4,512,1536]{2,1,0:T(8,128)(2,1)} %get-tuple-element.42.rows_hbm, ...), custom_call_target="tpu_custom_call" | custom-call | tf_op jit(solution)/shard_map/finish/pallas_call | solution.py:1701
  423.7 0.0 copy-start.1
  423.7 1.7 convert_reduce_fusion
  425.4 0.8 slice_convert_fusion.3
  426.2 0.7 copy.31
  426.9 2.0 slice_convert_fusion.1
  428.9 0.0 copy-start
  428.9 2.4 slice_convert_fusion
  431.3 2.2 convert_element_type.36
  433.5 0.0 copy-done.1
  433.5 2.5 convert_element_type.43
  435.9 0.0 copy-done
  435.9 0.0 copy-start.3
  435.9 4.2 convert_element_type.42
  440.1 0.0 copy-done.3
  440.1 0.7 copy.34
  440.9 0.0 copy-done.2
  440.9 0.7 copy.35
  (1 shorter events, 0.0 us)
Async XLA Ops:
  423.7 9.8 %copy-start.1 = (bf16[10,64,1536]{2,1,0:T(8,128)(2,1)S(1)}, bf16[10,64,1536]{2,1,0:T(8,128)(2,1)}, u32[]{:S(2)}) copy-start(bf16[10,64,1536]{2,1,0:T(8,128)(2,1)} %get-tuple-element.64) | copy-start | bytes 5898244
  428.9 7.0 %copy-start = (bf16[10,192,1024]{2,1,0:T(8,128)(2,1)S(1)}, bf16[10,192,1024]{2,1,0:T(8,128)(2,1)}, u32[]{:S(2)}) copy-start(bf16[10,192,1024]{2,1,0:T(8,128)(2,1)} %get-tuple-element.63) | copy-start | bytes 11796484
  435.9 4.2 copy-start.3
  435.9 5.0 %copy-start.2 = (bf16[128,1536]{1,0:T(8,128)(2,1)S(1)}, bf16[128,1536]{1,0:T(8,128)(2,1)}, u32[]{:S(2)}) copy-start(bf16[128,1536]{1,0:T(8,128)(2,1)} %get-tuple-element.103) | copy-start | bytes 1179652
where the time goes:
time: 448 us; the launch traced here: 442 us
  Pallas kernels  418 us (93%)
  other arithmetic  15.7 us (4%)
  local copies, waits for them, and re-layouts  7.5 us (2%)
    pallas_call x1, Pallas kernels, finish(): pl.pallas_call(functools.partial(finish_kernel, rows_y), name='finish', o...  168 us
    pallas_call x1, Pallas kernels, moe(): pl.pallas_call(functools.partial(moe_kernel, rows_y), name='moe', out_sha...  142 us
    pallas_call x1, Pallas kernels, gather(): pl.pallas_call(functools.partial(gather_kernel, rows_y, n // 12), name='g...  107 us

commit v1 on v0

--- a/solution.py
+++ b/solution.py
@@ -365,15 +365,15 @@
     ).astype(bf16)
     places = (iota((8, 128), 1) == iota((8, 128), 0) + EXPERTS) & (iota((8, 128), 0) < 2)
     columns = transposed(gain_rows, places.astype(f32).astype(bf16))
-    router = jnp.concatenate(
-        [w_router[...].astype(f32), jnp.zeros((n, 128 - EXPERTS), f32)], axis=1
-    )
+    shape = (w_router.shape[0], 128)
+    router = transposed(w_router[...], (iota(shape, 0) == iota(shape, 1)).astype(f32).astype(bf16))
     small_out[dp] = (router + columns).astype(bf16)
     lane, row = iota((length, 128), 1), iota((length, 128), 0)
-    chosen = routes[:, :1] == lane
-    for k in range(1, routes.shape[1]):
-        chosen = chosen | (routes[:, k : k + 1] == lane)
-    chosen = chosen.astype(f32)
+    chosen = routes[:1] == iota((128, length), 0)
+    for k in range(1, routes.shape[0]):
+        chosen = chosen | (routes[k : k + 1] == iota((128, length), 0))
+    same = (iota((128, 128), 0) == iota((128, 128), 1)).astype(f32).astype(bf16)
+    chosen = transposed(chosen.astype(f32).astype(bf16), same)
     dy_all[0, near, :width] = dy[...]
     dy_all[0, near, width:] = chosen.astype(bf16)
     greet([to[name] for name in ("z1", "z2", "y", "x", "c")])
@@ -608,7 +608,7 @@
 
 def gather(rows_y, weights, dy, *rest):
     w_down = rest[-1]
-    n, router_wide = weights[4].shape
+    n = weights[0].shape[0]
     dp_size = ZLINE * rows_y
     owned, _, width = w_down.shape
     hidden = F // ZLINE
@@ -624,7 +624,7 @@
 
     turned = jax.ShapeDtypeStruct((dp_size, 2, 2, n // 4, length), bf16)
     return pl.pallas_call(
-        functools.partial(gather_kernel, rows_y, n // 12),
+        functools.partial(gather_kernel, rows_y, n // 6),
         name="gather",
         out_shape=(
             jax.ShapeDtypeStruct((dp_size, n, qkv_wide), bf16),
@@ -711,6 +711,7 @@
     parts,
     heard_c,
     heard_x,
+    heard_z1,
     heard_z,
     combined,
     heard_combined,
@@ -789,6 +790,7 @@
     for load in loads:
         load.wait()
     x0.wait_recv()
+    z1_pair = links.copy(rows.at[0, pair], rows.at[1, pair], to["z1"])
     c0 = row_c(0)
     c0.wait_recv()
 
@@ -867,13 +869,19 @@
     def sum_x(r):
         made["c", r].wait_recv()
         parts[r, near] = add(parts.at[r, near], heard_c.at[r])
+        if r == 1:
+            made["z", 1] = links.copy(parts.at[1, near], heard_z1, to["z1"])
+            return
+        if r == 0:
+            made["z", 1].wait_recv()
+            parts[0, near] = add(parts.at[0, near], heard_z1)
         made["x", r] = links.copy(parts.at[r, pair], heard_x.at[r], to["x"])
 
     def sum_z(r):
         made["x", r].wait_recv()
         parts[r, own] = add(parts.at[r, own], heard_x.at[r])
         if r:
-            made["z", r] = links.copy(parts.at[r, own], heard_z.at[r - 1], to[f"z{r}"])
+            made["z", r] = links.copy(parts.at[r, own], heard_z.at[r - 2], to[f"z{r}"])
 
     def keep_combined(r):
         return pltpu.make_async_copy(
@@ -884,8 +892,6 @@
         slot = r % 2
         if r >= 2:
             made["oc", r - 2].wait_send()
-            keep_combined(r - 2).wait()
-            out_x(r - 2)
 
         def step(j, _):
             at = pl.ds(pl.multiple_of(j * 512, 512), 512)
@@ -957,14 +963,13 @@
         return 0
 
     forward(0)
-    z1.wait_recv()
-    x1 = row_x(1)
     z2.wait_recv()
     z3 = links.copy(rows.at[2, own], rows.at[3, own], to["z1"])
     x2 = row_x(2)
     load_down.wait()
     combine(0)
-    x1.wait_recv()
+    z1.wait_recv()
+    z1_pair.wait_recv()
     c1 = row_c(1)
     c1.wait_recv()
     forward(1)
@@ -980,7 +985,6 @@
     forward(2)
     backward(2)
     sum_c(2)
-    sum_z(1)
     x3.wait_recv()
     c3 = row_c(3)
     sum_x(2)
@@ -988,40 +992,45 @@
     forward(3)
     backward(3)
     sum_c(3)
-    backward(0)
-    sum_x(3)
-    sum_c(0)
-    sum_z(2)
+    keep_combined(0).wait()
+    out_x(0)
     for r in range(ZLINE):
         keep_rows(r).wait()
-    gathered = (z1, z2, z3, x0, x1, x2, x3, c0, c1, c2, c3)
+    gathered = (z1, z2, z3, z1_pair, x0, x2, x3, c0, c1, c2, c3)
     for copy in gathered:
         copy.wait_send()
     for r in range(ZLINE):
         fetch_dy(r).start()
-    sum_x(0)
-    combine(1)
+    sum_x(3)
+    sum_z(2)
     for r in range(ZLINE):
         fetch_dy(r).wait()
-    lax.fori_loop(0, 1, down, 0)
+    lax.fori_loop(0, 2, down, 0)
+    backward(0)
+    sum_c(0)
+    combine(1)
     sum_z(3)
+    sum_x(0)
+    lax.fori_loop(2, 3, down, 0)
     out_c(1)
-    lax.fori_loop(1, 2, down, 0)
     combine(2)
-    lax.fori_loop(2, 3, down, 0)
+    keep_combined(1).wait()
+    out_x(1)
     sum_z(0)
+    lax.fori_loop(3, 4, down, 0)
     out_c(2)
     combine(3)
-    lax.fori_loop(3, owned // 2, down, 0)
+    keep_combined(2).wait()
+    out_x(2)
+    lax.fori_loop(4, owned // 2, down, 0)
     out_c(3)
     total = parts[0, own].astype(f32)
-    for r in (1, 2, 3):
+    for r in (2, 3):
         made["z", r].wait_recv()
-        total = total + heard_z[r - 1].astype(f32)
+        total = total + heard_z[r - 2].astype(f32)
     total_ref[...] = total
-    for r in (2, 3):
-        keep_combined(r).wait()
-        out_x(r)
+    keep_combined(3).wait()
+    out_x(3)
     lax.fori_loop(0, owned, finish_down, 0)
     for r in range(ZLINE):
         made["ox", r].wait_recv()
@@ -1075,7 +1084,8 @@
             pltpu.VMEM((ZLINE, count, wide), bf16),
             pltpu.VMEM((ZLINE, count // 2, wide), bf16),
             pltpu.VMEM((ZLINE, length, wide), bf16),
-            pltpu.VMEM((ZLINE - 1, length, wide), bf16),
+            pltpu.VMEM((count // 2, wide), bf16),
+            pltpu.VMEM((ZLINE - 2, length, wide), bf16),
             pltpu.VMEM((2, count, width), bf16),
             pltpu.VMEM((ZLINE, count // 2, width), bf16),
             pltpu.VMEM((128, span), bf16),
@@ -1270,8 +1280,8 @@
         )
 
     class Sum:
-        def __init__(self, k, out, rows):
-            self.k, self.out, self.rows = k, out, rows
+        def __init__(self, k, out, rows, z_first=False):
+            self.k, self.out, self.rows, self.z_first = k, out, rows, z_first
             self.own, self.c, self.x, self.y, self.z1, self.z2 = refs[6 * k : 6 * k + 6]
 
         def copy(self, step, source, target, device):
@@ -1279,16 +1289,22 @@
                 source, target, a_send.at[self.k, step], a_recv.at[self.k, step], device
             )
 
+        def line(self, m):
+            if self.z_first:
+                return self.own.at[z_of[m], :, self.rows]
+            return self.own.at[z_of[m], y, self.rows]
+
+        def last_y(self):
+            return self.copy(8, self.own.at[z, 1 - y, self.rows], self.y.at[0], to["y"])
+
         def to_y(self, b):
             return self.copy(8 + b, self.own.at[b, 1 - y, self.rows], self.y.at[b], to["y"])
 
         def to_z1(self, m):
-            return self.copy(
-                1 + m, self.own.at[z_of[1 + 2 * m], y, self.rows], self.z1.at[m], to["z1"]
-            )
+            return self.copy(1 + m, self.line(1 + 2 * m), self.z1.at[m], to["z1"])
 
         def to_z2(self):
-            return self.copy(3, self.own.at[z_of[2], y, self.rows], self.z2, to["z2"])
+            return self.copy(3, self.line(2), self.z2, to["z2"])
 
         def back_x(self):
             return self.copy(4, self.out.at[mine], self.out.at[mine], to["x"])
@@ -1316,27 +1332,46 @@
                     self.own[b, k, self.rows] = add(self.own[b, k, self.rows], self.x[b, k])
             self.along_y()
 
+        def begin(self):
+            if self.z_first:
+                self.along_z()
+            else:
+                self.along_y()
+
         def along_y(self):
             for b in range(ZLINE):
                 self.to_y(b).start()
 
+        def along_z(self):
+            for m in (1, 0):
+                self.to_z1(m).start()
+
         def after_y(self):
+            if self.z_first:
+                self.last_y().wait_recv()
+                self.out[mine] = add(self.own[z, y, self.rows], self.y[0])
+                self.back_x().start()
+                return
             for b in range(ZLINE):
                 self.to_y(b).wait_recv()
                 self.own[b, y, self.rows] = add(self.own[b, y, self.rows], self.y[b])
-            for m in (1, 0):
-                self.to_z1(m).start()
+            self.along_z()
 
         def after_z1(self):
             for m in (1, 0):
                 self.to_z1(m).wait_recv()
-                at = z_of[2 * m]
-                self.own[at, y, self.rows] = add(self.own[at, y, self.rows], self.z1[m])
+                line = self.line(2 * m)
+                line[...] = add(line[...], self.z1[m])
                 if m:
                     self.to_z2().start()
 
         def after_z2(self):
             self.to_z2().wait_recv()
+            if self.z_first:
+                line = self.line(0)
+                line[...] = add(line[...], self.z2[...])
+                self.last_y().start()
+                return
             self.out[mine] = add(self.own[z, y, self.rows], self.z2[...])
             self.back_x().start()
 
@@ -1348,11 +1383,14 @@
             self.back_c().wait()
             for made in (self.to_z1(0), self.to_z1(1), self.to_z2(), self.back_x()):
                 made.wait_send()
+            if self.z_first:
+                self.last_y().wait_send()
+                return
             for b in range(ZLINE):
                 self.to_y(b).wait_send()
 
     whole = pl.ds(0, quarter)
-    output = Sum(0, out_0, whole)
+    output = Sum(0, out_0, whole, True)
     small = Sum(1, out_1, of_side)
     qkv = Sum(2, out_2, whole)
 
@@ -1366,7 +1404,7 @@
             return 0
 
         lax.fori_loop(0, right.shape[1] // 512, step, 0)
-        array.along_y()
+        array.begin()
 
     def load_output(i):
         step = w_output.shape[1]
@@ -1567,62 +1605,65 @@
 
         return 0
 
+    rights[2].wait_recv()
+    rights[3].start()
     lax.fori_loop(0, 1, gate_up, 0)
     send_y(0).start()
+    lax.fori_loop(0, KV // GROUP // 2, attend, 0)
     lax.fori_loop(1, 2, gate_up, 0)
     send_y(1).start()
-    rights[2].wait_recv()
-    rights[3].start()
+    lax.fori_loop(KV // GROUP // 2, KV // GROUP, attend, 0)
+    qkv_rights[2].start()
+    qkv_rights[1].start()
+    right_qkv[own_tokens] = grad_qkv[...]
     o_after_z1()
     for made in lefts:
         made.wait_recv()
     rights[1].wait_recv()
     rights[3].wait_recv()
     products(output, left_output, right_output)
-    lax.fori_loop(0, KV // GROUP // 2, attend, 0)
+    reduce(0)
     lax.fori_loop(2, 3, gate_up, 0)
     send_y(2).start()
-    reduce(0)
-    lax.fori_loop(KV // GROUP // 2, KV // GROUP, attend, 0)
-    qkv_rights[2].start()
-    qkv_rights[1].start()
     o_end()
-    right_qkv[own_tokens] = grad_qkv[...]
+    qkv_rights[2].wait_recv()
+    qkv_rights[3].start()
+    reduce(1)
     lax.fori_loop(3, 4, gate_up, 0)
     send_y(3).start()
-    reduce(1)
-    output.after_y()
-    input_grads()
-    lax.fori_loop(4, 5, gate_up, 0)
-    send_y(4).start()
-    qkv_rights[2].wait_recv()
-    qkv_rights[3].start()
-    reduce(2)
     qkv_rights[1].wait_recv()
     qkv_rights[3].wait_recv()
     products(qkv, left_qkv, right_qkv)
+    input_grads()
+    reduce(2)
+    lax.fori_loop(4, 5, gate_up, 0)
+    send_y(4).start()
     small.after_c()
+    output.after_z1()
     reduce(3)
-    output.after_z1()
-    lax.fori_loop(5, 7, gate_up, 0)
+    lax.fori_loop(5, 6, gate_up, 0)
     send_y(5).start()
+    lax.fori_loop(6, 7, gate_up, 0)
+    small.after_x()
     output.after_z2()
-    lax.fori_loop(7, owned, gate_up, 0)
-    small.after_x()
     reduce(4)
     send_y(6).start()
+    lax.fori_loop(7, 8, gate_up, 0)
     qkv.after_y()
+    reduce(5)
     send_y(7).start()
-    output.after_back()
-    reduce(5)
+    lax.fori_loop(8, 9, gate_up, 0)
+    lax.fori_loop(9, 10, gate_up, 0)
+    output.after_y()
+    qkv.after_z1()
+    reduce(6)
     send_y(8).start()
     small.after_y()
-    reduce(6)
+    reduce(7)
     send_y(9).start()
-    qkv.after_z1()
-    reduce(7)
+    qkv.after_z2()
+    output.after_back()
     small.after_z1()
-    qkv.after_z2()
     reduce(8)
     small.after_z2()
     qkv.after_back()
@@ -1687,15 +1728,16 @@
     vmem = pl.BlockSpec(memory_space=pltpu.VMEM)
     sems = pltpu.SemaphoreType.DMA
 
-    def summed(wide, own_rows):
+    def summed(wide, own_rows, z_first=False):
         heard = own_rows != n // 4
+        ends = (rows_y, n // 4, wide) if z_first else (n // 4, wide)
         return [
             pltpu.VMEM((ZLINE, rows_y, own_rows, wide), bf16),
             pltpu.VMEM((ZLINE, rows_y, n // 2, wide) if heard else (16, 128), bf16),
             pltpu.VMEM((ZLINE, rows_y, n // 4, wide) if heard else (16, 128), bf16),
-            pltpu.VMEM((ZLINE, n // 4, wide), bf16),
-            pltpu.VMEM((2, n // 4, wide), bf16),
-            pltpu.VMEM((n // 4, wide), bf16),
+            pltpu.VMEM((1 if z_first else ZLINE, n // 4, wide), bf16),
+            pltpu.VMEM((2,) + ends, bf16),
+            pltpu.VMEM(ends, bf16),
         ]
 
     return pl.pallas_call(
@@ -1733,7 +1775,7 @@
             pltpu.VMEM((length, width), f32),
             pltpu.VMEM((length, width), bf16),
             pltpu.VMEM((width, 128), f32),
-            *summed(columns[0], n // 4),
+            *summed(columns[0], n // 4, True),
             *summed(columns[1], n // 2),
             *summed(columns[2], n // 4),
             sems,
@@ -1756,6 +1798,65 @@
             collective_id=3, has_side_effects=True, vmem_limit_bytes=63 * 2**20
         ),
     )(rows, grads, combined, heard, w_output, w_qkv, *small)
+
+
+def widen_kernel(
+    gate_up,
+    down,
+    qkv,
+    output,
+    small,
+    tokens,
+    grad_tokens,
+    gate_up_out,
+    down_out,
+    query_out,
+    key_out,
+    value_out,
+    output_out,
+    router_out,
+    gains_out,
+    tokens_out,
+    grad_tokens_out,
+):
+    gate_up_out[...] = gate_up[...].astype(f32)
+    down_out[...] = down[...].astype(f32)
+
+    @pl.when(pl.program_id(0) == 0)
+    def _():
+        query_out[...] = qkv[:, : H * HD].astype(f32)
+        key_out[...] = qkv[:, H * HD : (H + KV) * HD].astype(f32)
+        value_out[...] = qkv[:, (H + KV) * HD :].astype(f32)
+        output_out[...] = output[...].astype(f32)
+        router_out[...] = small[:, :EXPERTS].astype(f32)
+        lane, row = (lax.broadcasted_iota(jnp.int32, (8, 128), k) for k in (1, 0))
+        gains_out[...] = against((lane == row + EXPERTS).astype(f32).astype(bf16), small[...])
+        tokens_out[...] = tokens[...]
+        grad_tokens_out[...] = grad_tokens[...]
+
+
+def widen(*sums):
+    gate_up, down, qkv, output, small, tokens, grad_tokens = sums
+    n = qkv.shape[0]
+
+    def whole(shape):
+        return pl.BlockSpec(shape, lambda e: (0,) * len(shape))
+
+    def one(shape):
+        return pl.BlockSpec((1,) + shape[1:], lambda e: (e, 0, 0))
+
+    shapes = [(n, H * HD), (n, KV * HD), (n, KV * HD), output.shape, (n, EXPERTS), (8, n)]
+    return pl.pallas_call(
+        widen_kernel,
+        name="widen",
+        grid=(gate_up.shape[0],),
+        out_shape=[jax.ShapeDtypeStruct(v, f32) for v in [gate_up.shape, down.shape] + shapes]
+        + [jax.ShapeDtypeStruct(tokens.shape, bf16)] * 2,
+        in_specs=[one(gate_up.shape), one(down.shape)] + [whole(v.shape) for v in sums[2:]],
+        out_specs=[one(gate_up.shape), one(down.shape)]
+        + [whole(v) for v in shapes + [tokens.shape] * 2],
+        compiler_params=pltpu.CompilerParams(vmem_limit_bytes=63 * 2**20),
+    )(*sums)
 
 
 def permuted(
@@ -2036,7 +2137,7 @@
         )
     length, width = tokens.shape
     per_group = H // KV
-    q_end, k_end, v_end = H * HD, (H + KV) * HD, (H + 2 * KV) * HD
+    v_end = (H + 2 * KV) * HD
 
     angles = np.arange(length)[:, None] * 10000.0 ** (-2.0 * np.arange(HD // 2) / HD)[None, :]
     repeats = (1, GROUP * per_group)
@@ -2061,11 +2162,11 @@
         allowed,
     ) = gather(
         place.rows_y,
-        (w_query, w_key, w_value, w_output, w_router, gain_attn[None, :], gain_moe[None, :]),
+        (w_query, w_key, w_value, w_output, w_router.T, gain_attn[None, :], gain_moe[None, :]),
         cotangent,
         tokens,
         segments,
-        routes,
+        routes.T,
         cosine,
         sine,
         w_down,
@@ -2099,18 +2200,30 @@
         cosine,
         sine,
     )
+    (
+        shard_gate_up,
+        shard_down,
+        shard_query,
+        shard_key,
+        shard_value,
+        shard_output,
+        shard_router,
+        shard_gains,
+        output,
+        grad_tokens,
+    ) = widen(shard_gate_up, shard_down, sum_qkv, sum_output, sum_small, output, grad_tokens)
     return (
         output,
         grad_tokens,
-        sum_qkv[:, :q_end].astype(f32),
-        sum_qkv[:, q_end:k_end].astype(f32),
-        sum_qkv[:, k_end:].astype(f32),
-        sum_output.astype(f32),
-        sum_small[:, :EXPERTS].astype(f32),
-        sum_small[:, EXPERTS].astype(f32),
-        sum_small[:, EXPERTS + 1].astype(f32),
-        shard_gate_up.astype(f32),
-        shard_down.astype(f32),
+        shard_query,
+        shard_key,
+        shard_value,
+        shard_output,
+        shard_router,
+        shard_gains[0],
+        shard_gains[1],
+        shard_gate_up,
+        shard_down,
     )
 
 

time: 448 us -> 430 us (0.960)
  other arithmetic: 15.7 us -> 0 us
    convert_element_type x7 -> x0, other arithmetic: 15.7 us -> none  [the longest x1 4.2 us: local(): shard_gate_up.astype(f32)]
    pallas_call x1 -> x2, Pallas kernels: 107 us -> 122 us  [the longest x1 110 us: gather(): pl.pallas_call(functools.partial(gather_kernel, rows_y, n // 6), name='ga...]
    pallas_call x1, Pallas kernels: 142 us -> 133 us  [moe(): pl.pallas_call(functools.partial(moe_kernel, rows_y), name='moe', out_sha...]
    pallas_call x1, Pallas kernels: 168 us -> 163 us  [finish(): pl.pallas_call(functools.partial(finish_kernel, rows_y), name='finish', o...]
where the time goes in v1:
time: 430 us; the launch traced here: 424 us
  Pallas kernels  418 us (97%)
  local copies, waits for them, and re-layouts  5.37 us (1%)
    pallas_call x1, Pallas kernels, finish(): pl.pallas_call(functools.partial(finish_kernel, rows_y), name='finish', o...  163 us
    pallas_call x1, Pallas kernels, moe(): pl.pallas_call(functools.partial(moe_kernel, rows_y), name='moe', out_sha...  133 us
    pallas_call x1, Pallas kernels, gather(): pl.pallas_call(functools.partial(gather_kernel, rows_y, n // 6), name='ga...  110 us
    pallas_call x1, Pallas kernels, widen(): pl.pallas_call(widen_kernel, name='widen', grid=(gate_up.shape[0],), out_...  11.7 us

profile of v1, /device:TPU:0, one launch (start us, length us, event | category | flops | bytes accessed | tf_op | source)
XLA Modules:
  0.0 424.1 jit_solution(8920846372740739182)
XLA Ops:
  0.6 1.2 broadcast_in_dim.6.gain_attn
  1.9 1.2 broadcast_in_dim.7.gain_moe
  3.1 109.9 %gather.1 = (bf16[8,192,2560]{2,1,0:T(8,128)(2,1)}, bf16[8,192,1536]{2,1,0:T(8,128)(2,1)}, bf16[4,512,1664]{2,1,0:T(8,128)(2,1)}, bf16[4,512,1280]{2,1,0:T(8,128...) custom-call(bf16[192,1536]{1,0:T(8,128)(2,1)} %w_query.1, ...), custom_call_target="tpu_custom_call" | custom-call | tf_op jit(solution)/shard_map/gather/pallas_call | solution.py:626
  113.0 132.8 %moe.1 = (bf16[4,512,1536]{2,1,0:T(8,128)(2,1)}, bf16[4,512,2560]{2,1,0:T(8,128)(2,1)}, bf16[10,64,1536]{2,1,0:T(8,128)(2,1)}, bf16[4,256,1536]{2,1,0:T(8,128)(2...) custom-call(bf16[128,1536]{1,0:T(8,128)(2,1)} %get-tuple-element.48.normed_ref.normed_moe, ...), custom_call_target="tpu_custom_call" | custom-call | tf_op jit(solution)/shard_map/moe/pallas_call | solution.py:1058
  245.8 163.4 %finish.1 = (bf16[10,192,1024]{2,1,0:T(8,128)(2,1)}, bf16[128,1536]{1,0:T(8,128)(2,1)}, bf16[128,1536]{1,0:T(8,128)(2,1)}, bf16[192,1536]{1,0:T(8,128)(2,1)}, bf...) custom-call(bf16[4,512,1536]{2,1,0:T(8,128)(2,1)} %get-tuple-element.52.rows_hbm, ...), custom_call_target="tpu_custom_call" | custom-call | tf_op jit(solution)/shard_map/finish/pallas_call | solution.py:1743
  409.2 11.7 %widen.1 = (f32[10,192,1024]{2,1,0:T(8,128)}, f32[10,64,1536]{2,1,0:T(8,128)}, f32[192,1536]{1,0:T(8,128)}, f32[192,512]{1,0:T(8,128)}, f32[192,512]{1,0:T(8,128...) custom-call(bf16[10,192,1024]{2,1,0:T(8,128)(2,1)} %get-tuple-elemen, ...), custom_call_target="tpu_custom_call" | custom-call | tf_op jit(solution)/shard_map/widen/pallas_call | solution.py:1849
  421.0 1.3 fusion
  422.3 1.6 copy.26

commit v2 on v1

--- a/solution.py
+++ b/solution.py
@@ -360,8 +360,8 @@
     line = iota((8, n), 0)
     gain_rows = jnp.where(
         line == 0,
-        gain_attn[...].astype(f32),
-        jnp.where(line == 1, gain_moe[...].astype(f32), 0.0),
+        gain_attn[...].astype(f32).reshape(1, n),
+        jnp.where(line == 1, gain_moe[...].astype(f32).reshape(1, n), 0.0),
     ).astype(bf16)
     places = (iota((8, 128), 1) == iota((8, 128), 0) + EXPERTS) & (iota((8, 128), 0) < 2)
     columns = transposed(gain_rows, places.astype(f32).astype(bf16))
@@ -1005,12 +1005,12 @@
     sum_z(2)
     for r in range(ZLINE):
         fetch_dy(r).wait()
-    lax.fori_loop(0, 2, down, 0)
     backward(0)
     sum_c(0)
+    lax.fori_loop(0, 2, down, 0)
+    sum_x(0)
     combine(1)
     sum_z(3)
-    sum_x(0)
     lax.fori_loop(2, 3, down, 0)
     out_c(1)
     combine(2)
@@ -2162,7 +2162,7 @@
         allowed,
     ) = gather(
         place.rows_y,
-        (w_query, w_key, w_value, w_output, w_router.T, gain_attn[None, :], gain_moe[None, :]),
+        (w_query, w_key, w_value, w_output, w_router.T, gain_attn, gain_moe),
         cotangent,
         tokens,
         segments,

time: 430 us -> 425 us (0.988)
  no operation moved by 1% of the time
where the time goes in v2:
time: 425 us; the launch traced here: 420 us
  Pallas kernels  416 us (98%)
    pallas_call x1, Pallas kernels, finish(): pl.pallas_call(functools.partial(finish_kernel, rows_y), name='finish', o...  164 us
    pallas_call x1, Pallas kernels, moe(): pl.pallas_call(functools.partial(moe_kernel, rows_y), name='moe', out_sha...  131 us
    pallas_call x1, Pallas kernels, gather(): pl.pallas_call(functools.partial(gather_kernel, rows_y, n // 6), name='ga...  110 us
    pallas_call x1, Pallas kernels, widen(): pl.pallas_call(widen_kernel, name='widen', grid=(gate_up.shape[0],), out_...  11.7 us

profile of v2, /device:TPU:0, one launch (start us, length us, event | category | flops | bytes accessed | tf_op | source)
XLA Modules:
  0.0 420.2 jit_solution(10949440974270829969)
XLA Ops:
  0.6 109.9 %gather.1 = (bf16[8,192,2560]{2,1,0:T(8,128)(2,1)}, bf16[8,192,1536]{2,1,0:T(8,128)(2,1)}, bf16[4,512,1664]{2,1,0:T(8,128)(2,1)}, bf16[4,512,1280]{2,1,0:T(8,128...) custom-call(bf16[192,1536]{1,0:T(8,128)(2,1)} %w_query.1, ...), custom_call_target="tpu_custom_call" | custom-call | tf_op jit(solution)/shard_map/gather/pallas_call | solution.py:626
  110.5 131.0 %moe.1 = (bf16[4,512,1536]{2,1,0:T(8,128)(2,1)}, bf16[4,512,2560]{2,1,0:T(8,128)(2,1)}, bf16[10,64,1536]{2,1,0:T(8,128)(2,1)}, bf16[4,256,1536]{2,1,0:T(8,128)(2...) custom-call(bf16[128,1536]{1,0:T(8,128)(2,1)} %get-tuple-element.48.normed_ref.normed_moe, ...), custom_call_target="tpu_custom_call" | custom-call | tf_op jit(solution)/shard_map/moe/pallas_call | solution.py:1058
  241.6 163.8 %finish.1 = (bf16[10,192,1024]{2,1,0:T(8,128)(2,1)}, bf16[128,1536]{1,0:T(8,128)(2,1)}, bf16[128,1536]{1,0:T(8,128)(2,1)}, bf16[192,1536]{1,0:T(8,128)(2,1)}, bf...) custom-call(bf16[4,512,1536]{2,1,0:T(8,128)(2,1)} %get-tuple-element.52.rows_hbm, ...), custom_call_target="tpu_custom_call" | custom-call | tf_op jit(solution)/shard_map/finish/pallas_call | solution.py:1743
  405.4 11.7 %widen.1 = (f32[10,192,1024]{2,1,0:T(8,128)}, f32[10,64,1536]{2,1,0:T(8,128)}, f32[192,1536]{1,0:T(8,128)}, f32[192,512]{1,0:T(8,128)}, f32[192,512]{1,0:T(8,128...) custom-call(bf16[10,192,1024]{2,1,0:T(8,128)(2,1)} %get-tuple-elemen, ...), custom_call_target="tpu_custom_call" | custom-call | tf_op jit(solution)/shard_map/widen/pallas_call | solution.py:1849
  417.1 1.3 fusion
  418.5 1.6 copy.26
